TPU v7x, 32 devices: a whole 2x2x4 slice. The times are simulated.
32 devices in a mesh: section: 4 (over y, core), dp: 8 (over z, x).
Axes of the slice: x: 2, y: 2, z: 4, core: 2. Of those that a mesh axis runs over, the one named last changes fastest.
Arguments:
- crop_maps: bfloat16 [8, 4, 2, 8, 8, 640], P('dp'), may hold values from -6 to 6
- target_maps: int32 [8, 4, 2, 8, 8], P('dp'), may hold values 0 or 1
- crop_counts: int32 [8, 4], P('dp'), may hold values from 1 to 2, as said below
- depth_kernels: float32 [4, 49, 640], P('section'), may hold values from -0.875 to 0.875
- weight_in: bfloat16 [4, 640, 2560], P('section', 'dp'), may hold values from -0.25 to 0.25
- weight_out: bfloat16 [4, 2560, 640], P('section', 'dp'), may hold values from -0.125 to 0.125
- head_weight: float32 [640], replicated, may hold values from -0.25 to 0.25
Outputs:
- grad_in: float32 [4, 640, 2560], P('section', 'dp')
- grad_out: float32 [4, 2560, 640], P('section', 'dp')
- grad_kernels: float32 [4, 49, 640], P('section')
- grad_head: float32 [640], replicated
- loss_value: float32 [], replicated
Inputs may be any that keep to these rules, and one draw needn't show every extreme that they name: `crop_counts`: every data group has some micro-batch with exactly 2 crops.
All inputs are finite; a program needn't handle non-finite values. No bound on the sum of `target_maps` on one device may be relied on, other than what follows from the above.
Results may differ from a plain program's by a relative error of at most 0.034.
Values may be sent and summed in bfloat16 or wider, within the bound.
A program may use at most 128 MiB of HBM per device.

v0:
```python
import jax
import jax.numpy as jnp
from jax import lax
from jax.sharding import PartitionSpec as P

EPSILON = 1e-06
SQRT_HALF = 0.7071067811865476
INV_ROOT_TWO_PI = 0.3989422804014327


def from_behind(value, axis, steps):
    count = lax.axis_size(axis)
    first, last = (max(0, -steps), min(count, count - steps))
    return lax.ppermute(value, axis, [(source, source + steps) for source in range(first, last)])


def depthwise(values, kernel):
    side = values.shape[1]
    padded = jnp.pad(values, ((0, 0), (3, 3), (3, 3), (0, 0)))
    result = jnp.zeros_like(values)
    for vertical in range(7):
        for across in range(7):
            result = (
                result
                + padded[:, vertical : vertical + side, across : across + side, :]
                * kernel[vertical * 7 + across]
            )
    return result


def depthwise_back(grads, kernel):
    side = grads.shape[1]
    padded = jnp.pad(grads, ((0, 0), (3, 3), (3, 3), (0, 0)))
    result = jnp.zeros_like(grads)
    for vertical in range(7):
        for across in range(7):
            result = (
                result
                + padded[:, 6 - vertical : 6 - vertical + side, 6 - across : 6 - across + side, :]
                * kernel[vertical * 7 + across]
            )
    return result


def kernel_grad(values, grads):
    side = values.shape[1]
    padded = jnp.pad(values, ((0, 0), (3, 3), (3, 3), (0, 0)))
    taps = []
    for vertical in range(7):
        for across in range(7):
            taps.append(
                jnp.sum(
                    padded[:, vertical : vertical + side, across : across + side, :] * grads,
                    axis=(0, 1, 2),
                )
            )
    return jnp.stack(taps, axis=0)


def block_parts(tiles, kernel, weight_in):
    width = tiles.shape[-1]
    widened = tiles.astype(jnp.float32)
    mixed = depthwise(widened, kernel).reshape(-1, width)
    centred = mixed - jnp.mean(mixed, axis=-1, keepdims=True)
    inverse = lax.rsqrt(jnp.mean(centred * centred, axis=-1, keepdims=True) + EPSILON)
    normed = centred * inverse
    normed_low = normed.astype(jnp.bfloat16)
    hidden = jnp.dot(normed_low, weight_in, preferred_element_type=jnp.float32)
    activated = (hidden * 0.5 * (1.0 + lax.erf(hidden * SQRT_HALF))).astype(jnp.bfloat16)
    return (widened, normed, inverse, normed_low, hidden, activated)


def block_forward(tiles, kernel, weight_in, weight_out):
    width = tiles.shape[-1]
    widened, normed, inverse, normed_low, hidden, activated = block_parts(tiles, kernel, weight_in)
    output = jnp.dot(activated, weight_out, preferred_element_type=jnp.float32)
    return (widened.reshape(-1, width) + output).astype(jnp.bfloat16).reshape(tiles.shape)


def block_backward(tiles, upstream, kernel, weight_in, weight_out):
    width = tiles.shape[-1]
    widened, normed, inverse, normed_low, hidden, activated = block_parts(tiles, kernel, weight_in)
    up_flat = upstream.reshape(-1, width)
    through = lax.dot_general(
        up_flat, weight_out, (((1,), (1,)), ((), ())), preferred_element_type=jnp.float32
    )
    slope = (
        0.5 * (1.0 + lax.erf(hidden * SQRT_HALF))
        + hidden * jnp.exp(-0.5 * hidden * hidden) * INV_ROOT_TWO_PI
    )
    hidden_grad = (through * slope).astype(jnp.bfloat16)
    normed_grad = lax.dot_general(
        hidden_grad, weight_in, (((1,), (1,)), ((), ())), preferred_element_type=jnp.float32
    )
    mixed_grad = inverse * (
        normed_grad
        - jnp.mean(normed_grad, axis=-1, keepdims=True)
        - normed * jnp.mean(normed_grad * normed, axis=-1, keepdims=True)
    )
    mixed_tiles = mixed_grad.reshape(tiles.shape)
    kernel_term = kernel_grad(widened, mixed_tiles)
    tile_grad = (upstream.astype(jnp.float32) + depthwise_back(mixed_tiles, kernel)).astype(
        jnp.bfloat16
    )
    return (tile_grad, kernel_term, normed_low, hidden_grad, activated, up_flat)


def outer_sum(left, right):
    return lax.dot_general(
        left, right, (((0,), (0,)), ((), ())), preferred_element_type=jnp.float32
    )


def head_terms(final, targets, live, head_weight, factor):
    widened = final.astype(jnp.float32)
    logits = jnp.sum(widened * head_weight, axis=-1)
    weight_live = live.astype(jnp.float32)[:, :, None, None]
    truth = targets.astype(jnp.float32)
    loss_term = jnp.sum(weight_live * (jax.nn.softplus(logits) - truth * logits)) * factor
    logit_grad = (jax.nn.sigmoid(logits) - truth) * weight_live * factor
    seeds = (logit_grad[..., None] * head_weight).astype(jnp.bfloat16)
    head_term = jnp.sum(logit_grad[..., None] * widened, axis=(0, 1, 2, 3))
    return (loss_term, seeds, head_term)


def body(crop_maps, target_maps, crop_counts, depth_kernels, weight_in, weight_out, head_weight):
    section_index = lax.axis_index("section")
    section_count = lax.axis_size("section")
    micro_count = crop_maps.shape[1]
    slot_count = crop_maps.shape[2]
    kernel = depth_kernels[0]
    live = jnp.arange(slot_count)[None, :] < crop_counts[0][:, None]
    entering = crop_maps[0] * live[:, :, None, None, None].astype(jnp.bfloat16)
    first_full, second_full = (
        lax.all_gather(weight_in[0], "dp", axis=0, tiled=True),
        lax.all_gather(weight_out[0], "dp", axis=0, tiled=True),
    )
    blank_tile = jnp.zeros(entering.shape[1:], jnp.bfloat16)
    ticks = micro_count + section_count - 1

    def forward_step(moment, carry):
        arrived, saved, final = carry
        micro = moment - section_index
        active = (micro >= 0) & (micro < micro_count)
        place = jnp.clip(micro, 0, micro_count - 1)
        own_tiles = lax.dynamic_index_in_dim(entering, place, 0, keepdims=False)
        current = jnp.where(section_index == 0, own_tiles, arrived)
        result = lax.cond(
            active,
            lambda tiles: block_forward(tiles, kernel, first_full, second_full),
            lambda tiles: jnp.zeros_like(tiles),
            current,
        )
        old_saved = lax.dynamic_index_in_dim(saved, place, 0, keepdims=False)
        saved = lax.dynamic_update_index_in_dim(
            saved, jnp.where(active, current, old_saved), place, 0
        )
        old_final = lax.dynamic_index_in_dim(final, place, 0, keepdims=False)
        final = lax.dynamic_update_index_in_dim(
            final, jnp.where(active, result, old_final), place, 0
        )
        arrived = from_behind(result, "section", 1)
        return (arrived, saved, final)

    _, saved, final = lax.fori_loop(
        0, ticks, forward_step, (blank_tile, jnp.zeros_like(entering), jnp.zeros_like(entering))
    )
    is_last = section_index == section_count - 1
    last_weight = is_last.astype(jnp.float32)
    factor = 1.0 / (micro_count * slot_count)
    loss_term, seeds, head_term = head_terms(final, target_maps[0], live, head_weight, factor)
    head_total, loss_total = lax.psum(
        (head_term * last_weight, loss_term * last_weight), ("section", "dp")
    )
    first_back, second_back = (
        lax.all_gather(weight_in[0], "dp", axis=0, tiled=True),
        lax.all_gather(weight_out[0], "dp", axis=0, tiled=True),
    )
    width = entering.shape[-1]
    expand = first_back.shape[1]
    extra_start = (jnp.zeros((width, expand), jnp.float32), jnp.zeros((expand, width), jnp.float32))

    def backward_step(moment, carry):
        arrived, kernel_acc, extra = carry
        micro = moment - (section_count - 1 - section_index)
        active = (micro >= 0) & (micro < micro_count)
        place = jnp.clip(micro, 0, micro_count - 1)
        own_seed = lax.dynamic_index_in_dim(seeds, place, 0, keepdims=False)
        upstream = jnp.where(is_last, own_seed, arrived)
        stored = lax.dynamic_index_in_dim(saved, place, 0, keepdims=False)

        def run_block(operands):
            grad_tiles, inputs, acc_kernel, acc_extra = operands
            tile_grad, kernel_term, normed_low, hidden_grad, activated, up_flat = block_backward(
                inputs, grad_tiles, kernel, first_back, second_back
            )
            new_extra = (
                acc_extra[0] + outer_sum(normed_low, hidden_grad),
                acc_extra[1] + outer_sum(activated, up_flat),
            )
            return (tile_grad, acc_kernel + kernel_term, new_extra)

        def skip_block(operands):
            return (jnp.zeros_like(operands[0]), operands[2], operands[3])

        tile_grad, kernel_acc, extra = lax.cond(
            active, run_block, skip_block, (upstream, stored, kernel_acc, extra)
        )
        arrived = from_behind(tile_grad, "section", -1)
        return (arrived, kernel_acc, extra)

    _, kernel_acc, extra = lax.fori_loop(
        0, ticks, backward_step, (blank_tile, jnp.zeros(kernel.shape, jnp.float32), extra_start)
    )
    first_part, second_part = (
        lax.psum_scatter(
            extra[0].astype(jnp.bfloat16), "dp", scatter_dimension=0, tiled=True
        ).astype(jnp.float32),
        lax.psum_scatter(
            extra[1].astype(jnp.bfloat16), "dp", scatter_dimension=0, tiled=True
        ).astype(jnp.float32),
    )
    kernel_total = lax.psum(kernel_acc.astype(jnp.bfloat16), "dp").astype(jnp.float32)
    return (first_part[None], second_part[None], kernel_total[None], head_total, loss_total)


def solution(mesh):
    return jax.shard_map(
        body,
        mesh=mesh,
        in_specs=(
            P("dp", None, None, None, None, None),
            P("dp", None, None, None, None),
            P("dp", None),
            P("section", None, None),
            P("section", "dp", None),
            P("section", "dp", None),
            P(),
        ),
        out_specs=(
            P("section", "dp", None),
            P("section", "dp", None),
            P("section", None, None),
            P(),
            P(),
        ),
        check_vma=False,
    )
```

profile of v0, /device:TPU:0, one launch (start us, length us, event | category | flops | bytes accessed | tf_op | source)
XLA Modules:
  0.0 875.9 jit_solution(5738213141442353138)
XLA Ops:
  10.5 64.4 %all-gather.5.cloned.1.call-done = bf16[1,640,2560]{2,1,0:T(8,128)(2,1)} async-done(((bf16[1,80,2560]{2,1,0:T(8,128)(2,1)}), bf16[1,640,2560]{2,1,0:T(8,128)(2,1)}) %all-gather.5.cloned.1.call-update) | async-done | bytes 3276816 | tf_op jit(solution)/shard_map/all_gather | solution.py:135
  74.9 62.8 %all-gather.7.cloned.1.call-done = bf16[1,2560,640]{2,1,0:T(8,128)(2,1)} async-done(((bf16[1,320,640]{2,1,0:T(8,128)(2,1)}), bf16[1,2560,640]{2,1,0:T(8,128)(2,1)}) %all-gather.7.cloned.1.call-update) | async-done | bytes 3276816 | tf_op jit(solution)/shard_map/all_gather | solution.py:136
  137.8 82.5 %while.40 = (s32[]{:T(128)}, bf16[2,8,8,640]{3,2,1,0:T(8,128)(2,1)S(1)}, bf16[4,2,8,8,640]{4,3,2,1,0:T(8,128)(2,1)S(1)}, bf16[4,2,8,8,640]{4,3,2,1,0:T(8,128)(2,...) while((s32[]{:T(128)}, ...), condition=%wide.region_5.6_spmd, body=%wide.region_0.5_spmd.sunk | while | flops 849510528 | bytes 12179750 | solution.py:165
  138.0 7.5 conditional.5
  141.3 4.2 fusion.2
  147.9 7.5 conditional.5
  151.3 4.2 fusion.2
  158.9 7.5 conditional.5
  162.3 4.2 fusion.2
  166.4 3.2 collective-permute-start
  170.7 7.5 conditional.5
  174.1 4.2 fusion.2
  178.3 5.6 collective-permute-start
  185.1 13.1 %collective-permute-start = (bf16[2,8,8,640]{3,2,1,0:T(8,128)(2,1)S(1)}, bf16[2,8,8,640]{3,2,1,0:T(8,128)(2,1)S(1)}, u32[]{:S(2)}, u32[]{:S(2)}) collective-permute-start(bf16[2,8,8,640]{3,2,1,0:T(8,128)(2,1)S(1)} %get-tuple-element.1143), channel_id=1, source_target_pairs={{0,8},{8,16},{16,24},{1,9},{9,17},{17,25},{2,10},{10,18},{18,26},{... | collective-permute-start | bytes 491528 | tf_op jit(solution)/shard_map/while/body/eval_jaxpr/ppermute | solution.py:14
  199.4 5.6 collective-permute-start
  206.2 13.1 %collective-permute-start = (bf16[2,8,8,640]{3,2,1,0:T(8,128)(2,1)S(1)}, bf16[2,8,8,640]{3,2,1,0:T(8,128)(2,1)S(1)}, u32[]{:S(2)}, u32[]{:S(2)}) collective-permute-start(bf16[2,8,8,640]{3,2,1,0:T(8,128)(2,1)S(1)} %get-tuple-element.1143), channel_id=1, source_target_pairs={{0,8},{8,16},{16,24},{1,9},{9,17},{17,25},{2,10},{10,18},{18,26},{... | collective-permute-start | bytes 491528 | tf_op jit(solution)/shard_map/while/body/eval_jaxpr/ppermute | solution.py:14
  222.7 3.1 broadcast_in_dim.59
  225.8 3.5 broadcast_in_dim.58
  229.4 476.9 %while.41 = (s32[]{:T(128)}, bf16[2,8,8,640]{3,2,1,0:T(8,128)(2,1)}, f32[49,640]{1,0:T(8,128)S(1)}, f32[640,2560]{1,0:T(8,128)}, f32[2560,640]{1,0:T(8,128)}, /*...) while((s32[]{:T(128)}, ...), condition=%wide.region_63.64_spmd.clone, body=%wide.region_7.63_spmd.clone.sunk | while | flops 2131804288 | bytes 130983528 | solution.py:212
  233.0 5.5 collective-permute-done.1
  242.2 6.8 collective-permute-done.1
  252.7 180.7 %collective-permute-done.1 = bf16[2,8,8,640]{3,2,1,0:T(8,128)(2,1)} collective-permute-done((bf16[2,8,8,640]{3,2,1,0:T(8,128)(2,1)}, bf16[2,8,8,640]{3,2,1,0:T(8,128)(2,1)}, u32[]{:S(2)}, u32[]{:S(2)}) %collective-permute-start.1) | collective-permute-done | bytes 163872 | tf_op jit(solution)/shard_map/while/body/eval_jaxpr/ppermute | solution.py:14
  435.1 60.4 %conditional.6 = (bf16[2,8,8,640]{3,2,1,0:T(8,128)(2,1)}, f32[49,640]{1,0:T(8,128)S(1)}, f32[640,2560]{1,0:T(8,128)}, f32[2560,640]{1,0:T(8,128)}) conditional(s32[]{:T(128)} %convert_element_type.175, (f32[49,640]{1,0:T(8,128)S(1)}, f32[640,2560]{1,0:T(8,128)}, f32[2560,640]{1,0:T(8,128)}) %tuple.249, (pred[]{:T(512)}, s32[]{:T(128)}, ...), branch_computations={%region_8.8_spmd, %region_9.62_spmd} | conditional | flops 2131148928 | bytes 129667864 | solution.py:206
  439.2 3.0 fusion.228
  474.5 7.9 stack.299
  484.2 7.2 convolution_add_fusion.1
  492.8 2.7 copy-done.1
  496.8 5.7 collective-permute-done.1
  504.1 60.4 %conditional.6 = (bf16[2,8,8,640]{3,2,1,0:T(8,128)(2,1)}, f32[49,640]{1,0:T(8,128)S(1)}, f32[640,2560]{1,0:T(8,128)}, f32[2560,640]{1,0:T(8,128)}) conditional(s32[]{:T(128)} %convert_element_type.175, (f32[49,640]{1,0:T(8,128)S(1)}, f32[640,2560]{1,0:T(8,128)}, f32[2560,640]{1,0:T(8,128)}) %tuple.249, (pred[]{:T(512)}, s32[]{:T(128)}, ...), branch_computations={%region_8.8_spmd, %region_9.62_spmd} | conditional | flops 2131148928 | bytes 129667864 | solution.py:206
  508.2 3.0 fusion.228
  543.5 7.9 stack.299
  553.3 7.2 convolution_add_fusion.1
  561.8 2.7 copy-done.1
  565.8 5.7 collective-permute-done.1
  573.2 60.4 %conditional.6 = (bf16[2,8,8,640]{3,2,1,0:T(8,128)(2,1)}, f32[49,640]{1,0:T(8,128)S(1)}, f32[640,2560]{1,0:T(8,128)}, f32[2560,640]{1,0:T(8,128)}) conditional(s32[]{:T(128)} %convert_element_type.175, (f32[49,640]{1,0:T(8,128)S(1)}, f32[640,2560]{1,0:T(8,128)}, f32[2560,640]{1,0:T(8,128)}) %tuple.249, (pred[]{:T(512)}, s32[]{:T(128)}, ...), branch_computations={%region_8.8_spmd, %region_9.62_spmd} | conditional | flops 2131148928 | bytes 129667864 | solution.py:206
  577.3 3.0 fusion.228
  612.6 7.9 stack.299
  622.3 7.2 convolution_add_fusion.1
  634.9 5.7 collective-permute-done.1
  642.2 60.4 %conditional.6 = (bf16[2,8,8,640]{3,2,1,0:T(8,128)(2,1)}, f32[49,640]{1,0:T(8,128)S(1)}, f32[640,2560]{1,0:T(8,128)}, f32[2560,640]{1,0:T(8,128)}) conditional(s32[]{:T(128)} %convert_element_type.175, (f32[49,640]{1,0:T(8,128)S(1)}, f32[640,2560]{1,0:T(8,128)}, f32[2560,640]{1,0:T(8,128)}) %tuple.249, (pred[]{:T(512)}, s32[]{:T(128)}, ...), branch_computations={%region_8.8_spmd, %region_9.62_spmd} | conditional | flops 2131148928 | bytes 129667864 | solution.py:206
  646.3 3.0 fusion.228
  681.6 7.9 stack.299
  691.4 7.2 convolution_add_fusion.1
  706.3 4.9 convert_element_type.133
  711.2 4.9 convert_element_type.134
  716.9 38.5 %psum.21 = bf16[1,49,640]{2,0,1:T(2,128)(2,1)S(1)} all-reduce(bf16[1,49,640]{2,0,1:T(2,128)(2,1)S(1)} %broadcast_in_dim.64), channel_id=1, replica_groups=mesh['section'=4,'dp'=8] {'dp'}, use_global_device_ids=true, to_apply=%region_66.67 | all-reduce | flops 31360 | bytes 125440 | tf_op jit(solution)/shard_map/psum | solution.py:223
  756.4 38.9 %all-reduce.3 = (f32[640]{0:T(1024)}, f32[]{:T(128)}) all-reduce(f32[640]{0:T(1024)S(1)} %broadcast_multiply_fusion.4, f32[]{:T(128)S(6)} %mul.2377), channel_id=1, replica_groups=mesh['section'=4,'dp'=8] {'section','dp'}, use_global_device_ids=true, to_apply=%region_68.69 | all-reduce | flops 641 | bytes 5128 | tf_op jit(solution)/shard_map/psum | solution.py:172
  797.3 70.1 %reduce-scatter.5.cloned.1.call-done = bf16[320,640]{1,0:T(8,128)(2,1)} async-done(((bf16[2560,640]{1,0:T(8,128)(2,1)}), bf16[320,640]{1,0:T(8,128)(2,1)}) %reduce-scatter.5.cloned.1.call-update) | async-done | bytes 409616 | tf_op jit(solution)/shard_map/reduce_scatter | solution.py:219
  (1082 shorter events, 221.1 us)
Async XLA Ops:
  7.2 67.7 %all-gather.5.cloned.1.call-start = ((), (), s32[]{:S(2)}) async-start(), calls=%async_computation.4 | async-start | bytes 3686400 | tf_op jit(solution)/shard_map/all_gather | solution.py:135
  7.9 129.8 %all-gather.7.cloned.1.call-start = ((), (), s32[]{:S(2)}) async-start(), calls=%async_computation.5 | async-start | bytes 3686400 | tf_op jit(solution)/shard_map/all_gather | solution.py:136
  8.7 786.7 %reduce-scatter.3.cloned.1.call-start = ((), (), s32[]{:S(2)}) async-start(), calls=%async_computation.2 | async-start | bytes 3686400 | tf_op jit(solution)/shard_map/reduce_scatter | solution.py:216
  137.8 83.5 %copy-start.84 = (s32[1,4,2,8,8]{4,3,2,1,0:T(8,128)S(1)}, s32[1,4,2,8,8]{4,3,2,1,0:T(8,128)}, u32[]{:S(2)}) copy-start(s32[1,4,2,8,8]{4,3,2,1,0:T(8,128)} %param.16) | copy-start | bytes 6148
  145.5 2.3 collective-permute-start
  155.5 3.3 collective-permute-start
  166.4 4.2 collective-permute-start
  178.3 6.6 collective-permute-start
  185.1 14.1 %collective-permute-start = (bf16[2,8,8,640]{3,2,1,0:T(8,128)(2,1)S(1)}, bf16[2,8,8,640]{3,2,1,0:T(8,128)(2,1)S(1)}, u32[]{:S(2)}, u32[]{:S(2)}) collective-permute-start(bf16[2,8,8,640]{3,2,1,0:T(8,128)(2,1)S(1)} %get-tuple-element.1143), channel_id=1, source_target_pairs={{0,8},{8,16},{16,24},{1,9},{9,17},{17,25},{2,10},{10,18},{18,26},{... | collective-permute-start | bytes 491528 | tf_op jit(solution)/shard_map/while/body/eval_jaxpr/ppermute | solution.py:14
  199.4 6.6 collective-permute-start
  206.2 14.1 %collective-permute-start = (bf16[2,8,8,640]{3,2,1,0:T(8,128)(2,1)S(1)}, bf16[2,8,8,640]{3,2,1,0:T(8,128)(2,1)S(1)}, u32[]{:S(2)}, u32[]{:S(2)}) collective-permute-start(bf16[2,8,8,640]{3,2,1,0:T(8,128)(2,1)S(1)} %get-tuple-element.1143), channel_id=1, source_target_pairs={{0,8},{8,16},{16,24},{1,9},{9,17},{17,25},{2,10},{10,18},{18,26},{... | collective-permute-start | bytes 491528 | tf_op jit(solution)/shard_map/while/body/eval_jaxpr/ppermute | solution.py:14
  231.7 6.8 collective-permute-start.1
  240.9 8.1 collective-permute-start.1
  251.4 182.0 %collective-permute-start.1 = (bf16[2,8,8,640]{3,2,1,0:T(8,128)(2,1)}, bf16[2,8,8,640]{3,2,1,0:T(8,128)(2,1)}, u32[]{:S(2)}, u32[]{:S(2)}) collective-permute-start(bf16[2,8,8,640]{3,2,1,0:T(8,128)(2,1)} %get-tuple-element.1041), channel_id=1, source_target_pairs={{8,0},{16,8},{24,16},{9,1},{17,9},{25,17},{10,2},{18,10},{26,18},{... | collective-permute-start | bytes 491528 | tf_op jit(solution)/shard_map/while/body/eval_jaxpr/ppermute | solution.py:14
  451.4 3.7 copy-start.4
  455.1 19.4 %copy-start.81 = (f32[1,640]{1,0:T(1,128)S(1)}, f32[1,640]{1,0:T(1,128)}, u32[]{:S(2)}) copy-start(f32[1,640]{1,0:T(1,128)} %stack.274) | copy-start | bytes 7684 | tf_op jit(solution)/shard_map/while/body/eval_jaxpr/cond
  482.4 9.0 %slice-start = ((s8[6553600]{0:T(1024)(128)(4,1)}), s8[4194304]{0:T(1024)(128)(4,1)S(1)}, s32[]{:S(2)}) async-start(s8[6553600]{0:T(1024)(128)(4,1)} %bitcast.136), calls=%async_computation.6 | async-start | bytes 8388608 | tf_op jit(solution)/shard_map/while/body/eval_jaxpr/cond
  484.2 7.2 slice-start.1
  484.2 7.2 copy-start.7
  484.2 7.2 copy-start.9
  491.4 4.1 copy-start.17
  495.5 6.9 collective-permute-start.1
  520.4 3.7 copy-start.4
  524.1 19.4 %copy-start.81 = (f32[1,640]{1,0:T(1,128)S(1)}, f32[1,640]{1,0:T(1,128)}, u32[]{:S(2)}) copy-start(f32[1,640]{1,0:T(1,128)} %stack.274) | copy-start | bytes 7684 | tf_op jit(solution)/shard_map/while/body/eval_jaxpr/cond
  551.5 9.0 %slice-start = ((s8[6553600]{0:T(1024)(128)(4,1)}), s8[4194304]{0:T(1024)(128)(4,1)S(1)}, s32[]{:S(2)}) async-start(s8[6553600]{0:T(1024)(128)(4,1)} %bitcast.136), calls=%async_computation.6 | async-start | bytes 8388608 | tf_op jit(solution)/shard_map/while/body/eval_jaxpr/cond
  553.3 7.2 slice-start.1
  553.3 7.2 copy-start.7
  553.3 7.2 copy-start.9
  560.5 4.1 copy-start.17
  564.5 6.9 collective-permute-start.1
  589.5 3.7 copy-start.4
  593.2 19.4 %copy-start.81 = (f32[1,640]{1,0:T(1,128)S(1)}, f32[1,640]{1,0:T(1,128)}, u32[]{:S(2)}) copy-start(f32[1,640]{1,0:T(1,128)} %stack.274) | copy-start | bytes 7684 | tf_op jit(solution)/shard_map/while/body/eval_jaxpr/cond
  620.5 9.0 %slice-start = ((s8[6553600]{0:T(1024)(128)(4,1)}), s8[4194304]{0:T(1024)(128)(4,1)S(1)}, s32[]{:S(2)}) async-start(s8[6553600]{0:T(1024)(128)(4,1)} %bitcast.136), calls=%async_computation.6 | async-start | bytes 8388608 | tf_op jit(solution)/shard_map/while/body/eval_jaxpr/cond
  622.3 7.2 slice-start.1
  622.3 7.2 copy-start.7
  622.3 7.2 copy-start.9
  629.5 4.1 copy-start.17
  633.6 6.9 collective-permute-start.1
  658.5 3.7 copy-start.4
  662.2 19.4 %copy-start.81 = (f32[1,640]{1,0:T(1,128)S(1)}, f32[1,640]{1,0:T(1,128)}, u32[]{:S(2)}) copy-start(f32[1,640]{1,0:T(1,128)} %stack.274) | copy-start | bytes 7684 | tf_op jit(solution)/shard_map/while/body/eval_jaxpr/cond
  689.6 9.0 %slice-start = ((s8[6553600]{0:T(1024)(128)(4,1)}), s8[4194304]{0:T(1024)(128)(4,1)S(1)}, s32[]{:S(2)}) async-start(s8[6553600]{0:T(1024)(128)(4,1)} %bitcast.136), calls=%async_computation.6 | async-start | bytes 8388608 | tf_op jit(solution)/shard_map/while/body/eval_jaxpr/cond
  691.4 7.2 slice-start.1
  691.4 7.2 copy-start.7
  691.4 7.2 copy-start.9
  698.6 4.1 copy-start.17
  702.6 3.6 collective-permute-start.1
  711.2 156.2 %reduce-scatter.5.cloned.1.call-start = ((), (), s32[]{:S(2)}) async-start(), calls=%async_computation.3 | async-start | bytes 3686400 | tf_op jit(solution)/shard_map/reduce_scatter | solution.py:219
  716.1 40.1 %copy-start.14 = (bf16[4,2,8,8,640]{4,3,2,1,0:T(8,128)(2,1)S(1)}, bf16[4,2,8,8,640]{4,3,2,1,0:T(8,128)(2,1)}, u32[]{:S(2)}) copy-start(bf16[4,2,8,8,640]{4,3,2,1,0:T(8,128)(2,1)} %copy-done.13) | copy-start | bytes 1966084
  (301 other events, 636.9 us)
Sparse Core Ops, SparseCore 0:
  10.2 64.6 all-gather.4
  77.1 60.5 all-gather.6
  711.3 75.8 reduce-scatter.2
  791.0 76.3 reduce-scatter.4
where the time goes:
time: 878 us; the launch traced here: 876 us
  waiting for transfers between devices  417 us (47%)
  local copies, waits for them, and re-layouts  147 us (17%)
  other arithmetic  97.5 us (11%)
  blocking collectives  77.4 us (9%)
  matrix products  63.1 us (7%)
  starting transfers between devices  53.4 us (6%)
  between operations  14.6 us (2%)
    ppermute x14, waiting for transfers between devices, from_behind(): lax.ppermute(value, axis, [(source, source + steps) for source in range(f...  219 us
    another operation x200, local copies, waits for them, and re-layouts, kernel_grad(): return jnp.stack(taps, axis=0)  105 us
    reduce_scatter x1, waiting for transfers between devices, body(): lax.psum_scatter(extra[1].astype(jnp.bfloat16), 'dp', scatter_dimension=0...  70.1 us
    all_gather x1, waiting for transfers between devices, body(): lax.all_gather(weight_in[0], 'dp', axis=0, tiled=True)  64.4 us
    all_gather x1, waiting for transfers between devices, body(): lax.all_gather(weight_out[0], 'dp', axis=0, tiled=True)  62.8 us
    ppermute x14, starting transfers between devices, from_behind(): lax.ppermute(value, axis, [(source, source + steps) for source in range(f...  53.2 us
    psum x1, blocking collectives, body(): lax.psum((head_term * last_weight, loss_term * last_weight), ('section',...  38.9 us
    psum x1, blocking collectives, body(): lax.psum(kernel_acc.astype(jnp.bfloat16), 'dp').astype(jnp.float32)  38.5 us
  transfers between devices with their start and end apart: 18, of which 17 were waited for; matrix products, arithmetic and copies ran while one was open for 1% of the time, Pallas kernels for 0%

commit v1 on v0

v1 whole, which is shorter than its diff:
```python
import functools

import jax
import jax.numpy as jnp
from jax import lax
from jax.experimental import pallas as pl
from jax.experimental.pallas import tpu as pltpu
from jax.sharding import PartitionSpec as P

EPSILON = 1e-06
SQRT_HALF = 0.7071067811865476
INV_ROOT_TWO_PI = 0.3989422804014327
MESH = pl.DeviceIdType.MESH
LANES = 128
CHUNK = 512
TAPS = 7
SIDE = 8
SMALL_ROWS = 64
HEAD_ROW = 56


def shift_columns(values, distance):
    if distance == 0:
        return values
    column = lax.broadcasted_iota(jnp.int32, values.shape, 2)
    moved = pltpu.roll(values, (-distance) % SIDE, 2)
    keep = (column + distance >= 0) & (column + distance < SIDE)
    return jnp.where(keep, moved, 0.0)


def valid_rows(offset):
    return range(max(0, -offset), min(SIDE, SIDE - offset))


def depthwise(values, taps_ref, lanes, flip):
    rows = [jnp.zeros_like(values[:, 0]) for _ in range(SIDE)]
    for across in range(TAPS):
        shifted = shift_columns(values, across - 3)
        for vertical in range(TAPS):
            tap = vertical * TAPS + across
            if flip:
                tap = TAPS * TAPS - 1 - tap
            weight = taps_ref[pl.ds(tap, 1), lanes].reshape(1, 1, LANES)
            for row in valid_rows(vertical - 3):
                rows[row] = rows[row] + shifted[:, row + vertical - 3] * weight
    return jnp.stack(rows, axis=1)


def lane_tile(index):
    return pl.ds(pl.multiple_of(index * LANES, LANES), LANES)


def kernel(
    section_count, micro_count, slots,
    x_ref, target_ref, live_ref, taps_ref, first_ref, second_ref, head_ref,
    grad_in_ref, grad_out_ref, small_ref,
    tiles, results, ups, tile_grads, mixed, normed, normed_low, inverse, activated, slope,
    hidden_grad, kernel_acc, head_block,
    tile_send, tile_recv, up_send, up_recv, head_send, head_recv,
):
    section = lax.axis_index("section")
    last = section_count - 1
    cells = slots * SIDE * SIDE
    width = x_ref.shape[-1]
    expand = first_ref.shape[1]
    lane_tiles = width // LANES
    is_first = section == 0
    is_last = section == last
    following = jnp.minimum(section + 1, last)
    previous = jnp.maximum(section - 1, 0)

    barrier = pltpu.get_barrier_semaphore()
    for step in range(1, section_count):
        peer = lax.rem(section + step, section_count)
        pl.semaphore_signal(barrier, inc=1, device_id={"section": peer}, device_id_type=MESH)
    pl.semaphore_wait(barrier, section_count - 1)

    def rows_of(micro):
        return pl.ds(pl.multiple_of(micro * cells, cells), cells)

    def tile_copy(micro):
        return pltpu.make_async_remote_copy(
            src_ref=results.at[micro], dst_ref=tiles.at[micro],
            send_sem=tile_send.at[micro], recv_sem=tile_recv.at[micro],
            device_id={"section": following}, device_id_type=MESH,
        )

    def up_copy(micro):
        return pltpu.make_async_remote_copy(
            src_ref=tile_grads.at[micro], dst_ref=ups.at[micro],
            send_sem=up_send.at[micro], recv_sem=up_recv.at[micro],
            device_id={"section": previous}, device_id_type=MESH,
        )

    def head_copy(step):
        peer = lax.rem(section + step, section_count)
        return pltpu.make_async_remote_copy(
            src_ref=head_block, dst_ref=head_block,
            send_sem=head_send.at[step - 1], recv_sem=head_recv,
            device_id={"section": peer}, device_id_type=MESH,
        )

    @pl.when(is_last)
    def _():
        head_block[...] = jnp.zeros_like(head_block)

    def forward(micro, carry):
        @pl.when(is_first)
        def _():
            tiles[micro] = x_ref[micro]

        @pl.when(jnp.logical_not(is_first))
        def _():
            tile_copy(micro).wait_recv()

        def mix(index, carry):
            lanes = lane_tile(index)
            values = tiles[micro, :, lanes].astype(jnp.float32)
            values = values.reshape(slots, SIDE, SIDE, LANES)
            mixed[:, lanes] = depthwise(values, taps_ref, lanes, False).reshape(cells, LANES)
            return carry

        lax.fori_loop(0, lane_tiles, mix, 0)
        rows = rows_of(micro)
        value = mixed[...]
        centred = value - jnp.mean(value, axis=-1, keepdims=True)
        scale = lax.rsqrt(jnp.mean(centred * centred, axis=-1, keepdims=True) + EPSILON)
        unit = centred * scale
        low = unit.astype(jnp.bfloat16)
        normed[rows, :] = unit
        normed_low[rows, :] = low
        inverse[rows, :] = jnp.broadcast_to(scale, (cells, LANES))
        total = tiles[micro].astype(jnp.float32)
        for start in range(0, expand, CHUNK):
            columns = slice(start, start + CHUNK)
            hidden = jnp.dot(low, first_ref[:, columns], preferred_element_type=jnp.float32)
            portion = 0.5 * (1.0 + lax.erf(hidden * SQRT_HALF))
            active = (hidden * portion).astype(jnp.bfloat16)
            activated[rows, columns] = active
            slope[rows, columns] = (
                portion + hidden * jnp.exp(-0.5 * hidden * hidden) * INV_ROOT_TWO_PI
            )
            total = total + jnp.dot(
                active, second_ref[columns, :], preferred_element_type=jnp.float32
            )
        results[micro] = total.astype(jnp.bfloat16)

        @pl.when(jnp.logical_not(is_last))
        def _():
            tile_copy(micro).start()

        @pl.when(is_last)
        def _():
            final = results[micro].astype(jnp.float32)
            logits = jnp.sum(final * head_ref[...], axis=-1, keepdims=True)
            weight = live_ref[micro]
            truth = target_ref[micro]
            factor = 1.0 / (micro_count * slots)
            softplus = jnp.maximum(logits, 0.0) + jnp.log1p(jnp.exp(-jnp.abs(logits)))
            loss = jnp.sum(weight * (softplus - truth * logits)) * factor
            logit_grad = (1.0 / (1.0 + jnp.exp(-logits)) - truth) * weight * factor
            ups[micro] = (logit_grad * head_ref[...]).astype(jnp.bfloat16)
            term = jnp.sum(logit_grad * final, axis=0, keepdims=True)
            head_block[0:1, :] += term
            head_block[1:2, :] += jnp.full((1, width), loss)

        return carry

    lax.fori_loop(0, micro_count, forward, 0)

    @pl.when(is_last)
    def _():
        for step in range(1, section_count):
            head_copy(step).start()

    def backward(micro, carry):
        @pl.when(jnp.logical_not(is_last))
        def _():
            up_copy(micro).wait_recv()

        rows = rows_of(micro)
        upstream = ups[micro]
        total = jnp.zeros((cells, width), jnp.float32)
        for start in range(0, expand, CHUNK):
            columns = slice(start, start + CHUNK)
            through = lax.dot_general(
                upstream, second_ref[columns, :], (((1,), (1,)), ((), ())),
                preferred_element_type=jnp.float32,
            )
            grad = (through * slope[rows, columns]).astype(jnp.bfloat16)
            hidden_grad[rows, columns] = grad
            total = total + lax.dot_general(
                grad, first_ref[:, columns], (((1,), (1,)), ((), ())),
                preferred_element_type=jnp.float32,
            )
        unit = normed[rows, :]
        mixed_grad = inverse[rows, 0:1] * (
            total
            - jnp.mean(total, axis=-1, keepdims=True)
            - unit * jnp.mean(total * unit, axis=-1, keepdims=True)
        )
        normed[rows, :] = mixed_grad

        def unmix(index, carry):
            lanes = lane_tile(index)
            values = normed[rows, lanes].reshape(slots, SIDE, SIDE, LANES)
            back = depthwise(values, taps_ref, lanes, True).reshape(cells, LANES)
            back = back + ups[micro, :, lanes].astype(jnp.float32)
            tile_grads[micro, :, lanes] = back.astype(jnp.bfloat16)
            return carry

        @pl.when(jnp.logical_not(is_first))
        def _():
            lax.fori_loop(0, lane_tiles, unmix, 0)
            up_copy(micro).start()

        return carry

    lax.fori_loop(0, micro_count, backward, 0)

    upstreams = ups[...].reshape(micro_count * cells, width)
    for start in range(0, expand, CHUNK):
        columns = slice(start, start + CHUNK)
        grad_out_ref[columns, :] = lax.dot_general(
            activated[:, columns], upstreams, (((0,), (0,)), ((), ())),
            preferred_element_type=jnp.float32,
        ).astype(jnp.bfloat16)
    for start in range(0, expand, CHUNK):
        columns = slice(start, start + CHUNK)
        grad_in_ref[:, columns] = lax.dot_general(
            normed_low[...], hidden_grad[:, columns], (((0,), (0,)), ((), ())),
            preferred_element_type=jnp.float32,
        ).astype(jnp.bfloat16)

    kernel_acc[...] = jnp.zeros_like(kernel_acc)

    def tap_grads(flat, carry):
        micro = flat // lane_tiles
        lanes = lane_tile(flat % lane_tiles)
        values = tiles[micro, :, lanes].astype(jnp.float32)
        values = values.reshape(slots, SIDE, SIDE, LANES)
        grads = normed[rows_of(micro), lanes].reshape(slots, SIDE, SIDE, LANES)
        for across in range(TAPS):
            shifted = shift_columns(values, across - 3)
            for vertical in range(TAPS):
                offset = vertical - 3
                low, high = max(0, -offset), min(SIDE, SIDE - offset)
                product = shifted[:, low + offset : high + offset] * grads[:, low:high]
                kernel_acc[vertical * TAPS + across, :, lanes] += jnp.sum(product, axis=(0, 1))
        return carry

    lax.fori_loop(0, micro_count * lane_tiles, tap_grads, 0)
    small_ref[0:HEAD_ROW, :] = jnp.sum(kernel_acc[...], axis=1)

    @pl.when(is_last)
    def _():
        for step in range(1, section_count):
            head_copy(step).wait_send()

    @pl.when(jnp.logical_not(is_last))
    def _():
        head_copy(1).wait_recv()

    small_ref[HEAD_ROW:SMALL_ROWS, :] = head_block[...]

    def finish(micro, carry):
        @pl.when(jnp.logical_not(is_last))
        def _():
            tile_copy(micro).wait_send()

        @pl.when(jnp.logical_not(is_first))
        def _():
            up_copy(micro).wait_send()

        return carry

    lax.fori_loop(0, micro_count, finish, 0)


def body(crop_maps, target_maps, crop_counts, depth_kernels, weight_in, weight_out, head_weight):
    section_count = lax.axis_size("section")
    micro_count, slots = crop_maps.shape[1:3]
    width = crop_maps.shape[-1]
    cells = slots * SIDE * SIDE
    expand = weight_in.shape[2]
    live = jnp.arange(slots)[None, :] < crop_counts[0][:, None]
    entering = crop_maps[0] * live[:, :, None, None, None].astype(jnp.bfloat16)
    entering = entering.reshape(micro_count, cells, width)
    targets = target_maps[0].reshape(micro_count, cells, 1).astype(jnp.float32)
    weights = jnp.broadcast_to(
        live[:, :, None].astype(jnp.float32), (micro_count, slots, SIDE * SIDE)
    ).reshape(micro_count, cells, 1)
    first_full = lax.all_gather(weight_in[0], "dp", axis=0, tiled=True)
    second_full = lax.all_gather(weight_out[0], "dp", axis=0, tiled=True)
    low, full = jnp.bfloat16, jnp.float32
    every = micro_count * cells
    in_vmem = pl.BlockSpec(memory_space=pltpu.VMEM)
    grad_in, grad_out, small = pl.pallas_call(
        functools.partial(kernel, section_count, micro_count, slots),
        out_shape=(
            jax.ShapeDtypeStruct((width, expand), low),
            jax.ShapeDtypeStruct((expand, width), low),
            jax.ShapeDtypeStruct((SMALL_ROWS, width), full),
        ),
        in_specs=[in_vmem] * 7,
        out_specs=(in_vmem,) * 3,
        scratch_shapes=[
            pltpu.VMEM((micro_count, cells, width), low),
            pltpu.VMEM((micro_count, cells, width), low),
            pltpu.VMEM((micro_count, cells, width), low),
            pltpu.VMEM((micro_count, cells, width), low),
            pltpu.VMEM((cells, width), full),
            pltpu.VMEM((every, width), full),
            pltpu.VMEM((every, width), low),
            pltpu.VMEM((every, LANES), full),
            pltpu.VMEM((every, expand), low),
            pltpu.VMEM((every, expand), full),
            pltpu.VMEM((every, expand), low),
            pltpu.VMEM((HEAD_ROW, SIDE, width), full),
            pltpu.VMEM((SMALL_ROWS - HEAD_ROW, width), full),
            pltpu.SemaphoreType.DMA((micro_count,)),
            pltpu.SemaphoreType.DMA((micro_count,)),
            pltpu.SemaphoreType.DMA((micro_count,)),
            pltpu.SemaphoreType.DMA((micro_count,)),
            pltpu.SemaphoreType.DMA((section_count - 1,)),
            pltpu.SemaphoreType.DMA,
        ],
        compiler_params=pltpu.CompilerParams(
            collective_id=0, has_side_effects=True, vmem_limit_bytes=56 * 1024 * 1024
        ),
        cost_estimate=pl.CostEstimate(
            flops=12 * every * width * expand, bytes_accessed=8 * width * expand, transcendentals=0
        ),
    )(entering, targets, weights, depth_kernels[0], first_full, second_full, head_weight[None])
    grad_in_part = lax.psum_scatter(grad_in, "dp", scatter_dimension=0, tiled=True)
    grad_out_part = lax.psum_scatter(grad_out, "dp", scatter_dimension=0, tiled=True)
    small_total = lax.psum(small, "dp")
    taps = depth_kernels.shape[1]
    return (
        grad_in_part.astype(full)[None],
        grad_out_part.astype(full)[None],
        small_total[:taps][None],
        small_total[HEAD_ROW],
        small_total[HEAD_ROW + 1, 0],
    )


def solution(mesh):
    return jax.shard_map(
        body,
        mesh=mesh,
        in_specs=(
            P("dp", None, None, None, None, None),
            P("dp", None, None, None, None),
            P("dp", None),
            P("section", None, None),
            P("section", "dp", None),
            P("section", "dp", None),
            P(),
        ),
        out_specs=(
            P("section", "dp", None),
            P("section", "dp", None),
            P("section", None, None),
            P(),
            P(),
        ),
        check_vma=False,
    )
```

time: 878 us -> 449 us (0.51)
  local copies, waits for them, and re-layouts: 147 us -> 9.07 us
  other arithmetic: 97.5 us -> 7.46 us
  blocking collectives: 77.4 us -> 0 us
  Pallas kernels: 0 us -> 76.4 us
  waiting for transfers between devices: 417 us -> 341 us
  matrix products: 63.1 us -> 0 us
  starting transfers between devices: 53.4 us -> 0.19 us
    ppermute x14 -> x0, waiting for transfers between devices: 219 us -> none  [from_behind(): lax.ppermute(value, axis, [(source, source + steps) for source in range(f...]
    another operation x210 -> x0, local copies, waits for them, and re-layouts: 108 us -> none  [the longest x200 105 us: kernel_grad(): return jnp.stack(taps, axis=0)]
    reduce_scatter x2, waiting for transfers between devices: 70.1 us -> 152 us  [the longest x1 76.6 us: body(): lax.psum_scatter(grad_in, 'dp', scatter_dimension=0, tiled=True)]
    psum x2 -> x0, blocking collectives: 77.4 us -> none  [the longest x1 38.9 us: body(): lax.psum((head_term * last_weight, loss_term * last_weight), ('section',...]
    pallas_call x0 -> x1, Pallas kernels: none -> 76.4 us  [body(): pl.pallas_call(functools.partial(kernel, section_count, micro_count, slot...]
    psum x0 -> x1, waiting for transfers between devices: none -> 66 us  [body(): small_total = lax.psum(small, 'dp')]
    dot_general x24 -> x0, matrix products: 63.1 us -> none  [the longest x8 33.9 us: outer_sum(): lax.dot_general(left, right, (((0,), (0,)), ((), ())), preferred_element_...]
    ppermute x14 -> x0, starting transfers between devices: 53.2 us -> none  [from_behind(): lax.ppermute(value, axis, [(source, source + steps) for source in range(f...]
  transfers between devices with their start and end apart: 18 -> 5, of which waited for: 17 -> 5; matrix products, arithmetic and copies ran while one was open for 1% -> 3% of each run, Pallas kernels for 0% -> 0%
where the time goes in v1:
time: 449 us; the launch traced here: 448 us
  waiting for transfers between devices  341 us (76%)
  Pallas kernels  76.4 us (17%)
  between operations  13.8 us (3%)
  local copies, waits for them, and re-layouts  9.07 us (2%)
  other arithmetic  7.46 us (2%)
    reduce_scatter x1, waiting for transfers between devices, body(): lax.psum_scatter(grad_in, 'dp', scatter_dimension=0, tiled=True)  76.6 us
    pallas_call x1, Pallas kernels, body(): pl.pallas_call(functools.partial(kernel, section_count, micro_count, slot...  76.4 us
    reduce_scatter x1, waiting for transfers between devices, body(): lax.psum_scatter(grad_out, 'dp', scatter_dimension=0, tiled=True)  75.7 us
    psum x1, waiting for transfers between devices, body(): small_total = lax.psum(small, 'dp')  66 us
    all_gather x1, waiting for transfers between devices, body(): second_full = lax.all_gather(weight_out[0], 'dp', axis=0, tiled=True)  62.8 us
    all_gather x1, waiting for transfers between devices, body(): first_full = lax.all_gather(weight_in[0], 'dp', axis=0, tiled=True)  57.8 us
  transfers between devices with their start and end apart: 5, of which 5 were waited for; matrix products, arithmetic and copies ran while one was open for 3% of the time, Pallas kernels for 0%

profile of v1, /device:TPU:0, one launch (start us, length us, event | category | flops | bytes accessed | tf_op | source)
XLA Modules:
  0.0 448.1 jit_solution(17460734884884345177)
XLA Ops:
  7.2 0.0 all-gather.5.cloned.1.call-start
  7.2 0.7 all-gather.5.cloned.1.call-update
  7.9 0.0 all-gather.7.cloned.1.call-start
  7.9 0.7 all-gather.7.cloned.1.call-update
  8.6 0.0 all-reduce.2.cloned.1.call-start
  8.7 1.3 broadcast_in_dim.27.head_ref
  10.0 0.7 fusion
  10.7 0.1 mul.13
  10.8 0.1 mul.14
  10.9 0.8 convert_element_type.24
  11.6 1.6 copy.18
  13.2 0.8 convert_element_type.27.target_ref
  14.0 0.1 broadcast_in_dim.26
  14.1 0.9 reshape.85.live_ref
  15.0 2.1 broadcast_multiply_fusion.x_ref
  17.1 57.8 %all-gather.5.cloned.1.call-done = bf16[1,640,2560]{2,1,0:T(8,128)(2,1)} async-done(((bf16[1,80,2560]{2,1,0:T(8,128)(2,1)}), bf16[1,640,2560]{2,1,0:T(8,128)(2,1)}) %all-gather.5.cloned.1.call-update) | async-done | bytes 3276816 | tf_op jit(solution)/shard_map/all_gather | solution.py:293
  74.9 62.8 %all-gather.7.cloned.1.call-done = bf16[1,2560,640]{2,1,0:T(8,128)(2,1)} async-done(((bf16[1,320,640]{2,1,0:T(8,128)(2,1)}), bf16[1,2560,640]{2,1,0:T(8,128)(2,1)}) %all-gather.7.cloned.1.call-update) | async-done | bytes 3276816 | tf_op jit(solution)/shard_map/all_gather | solution.py:294
  137.7 76.4 %shard_map.110 = (bf16[640,2560]{1,0:T(8,128)(2,1)}, bf16[2560,640]{1,0:T(8,128)(2,1)}, f32[64,640]{1,0:T(8,128)}) custom-call(bf16[4,128,640]{2,1,0:T(8,128)(2,1)} %broadcast_multiply_fusion.x_ref, f32[4,128,1]{2,1,0:T(8,128)} %convert_element_type.27.target_ref, f32[4,128,1]{2,1,0:T(8,128)} %reshape.85.live_ref, f32[49,640]{1,0:T(8,128)} %bitcast.21, ...), custom_call_target="tpu_custom_call" | custom-call | flops 10066329600 | bytes 13107200 | tf_op jit(solution)/shard_map/pallas_call | solution.py:298
  214.0 0.0 all-reduce.2.cloned.1.call-update
  214.1 0.0 reduce-scatter.5.cloned.1.call-start
  214.1 0.5 reduce-scatter.5.cloned.1.call-update
  214.6 0.0 reduce-scatter.3.cloned.1.call-start
  214.7 0.5 reduce-scatter.3.cloned.1.call-update
  215.2 66.0 %all-reduce.2.cloned.1.call-done = f32[64,640]{1,0:T(8,128)} async-done(((f32[64,640]{1,0:T(8,128)}), f32[64,640]{1,0:T(8,128)}) %all-reduce.2.cloned.1.call-update) | async-done | bytes 163856 | tf_op jit(solution)/shard_map/psum | solution.py:337
  281.2 0.9 slice_bitcast_fusion
  282.2 0.8 copy.15
  282.9 1.2 slice.14
  284.1 1.3 slice_reduce_fusion
  285.4 75.7 %reduce-scatter.5.cloned.1.call-done = bf16[320,640]{1,0:T(8,128)(2,1)} async-done(((bf16[2560,640]{1,0:T(8,128)(2,1)}), bf16[320,640]{1,0:T(8,128)(2,1)}) %reduce-scatter.5.cloned.1.call-update) | async-done | bytes 409616 | tf_op jit(solution)/shard_map/reduce_scatter | solution.py:336
  361.1 1.9 bitcast_convert_fusion
  363.1 76.6 %reduce-scatter.3.cloned.1.call-done = bf16[80,2560]{1,0:T(8,128)(2,1)} async-done(((bf16[640,2560]{1,0:T(8,128)(2,1)}), bf16[80,2560]{1,0:T(8,128)(2,1)}) %reduce-scatter.3.cloned.1.call-update) | async-done | bytes 409616 | tf_op jit(solution)/shard_map/reduce_scatter | solution.py:335
  439.7 2.0 bitcast_convert_fusion.1
Async XLA Ops:
  7.2 67.7 %all-gather.5.cloned.1.call-start = ((), (), s32[]{:S(2)}) async-start(), calls=%async_computation.5 | async-start | bytes 3686400 | tf_op jit(solution)/shard_map/all_gather | solution.py:293
  7.9 129.8 %all-gather.7.cloned.1.call-start = ((), (), s32[]{:S(2)}) async-start(), calls=%async_computation.6 | async-start | bytes 3686400 | tf_op jit(solution)/shard_map/all_gather | solution.py:294
  8.6 272.6 %all-reduce.2.cloned.1.call-start = ((), (), s32[]{:S(2)}) async-start(), calls=%async_computation.4 | async-start | bytes 327680 | tf_op jit(solution)/shard_map/psum | solution.py:337
  214.1 147.1 %reduce-scatter.5.cloned.1.call-start = ((), (), s32[]{:S(2)}) async-start(), calls=%async_computation.3 | async-start | bytes 3686400 | tf_op jit(solution)/shard_map/reduce_scatter | solution.py:336
  214.6 225.0 %reduce-scatter.3.cloned.1.call-start = ((), (), s32[]{:S(2)}) async-start(), calls=%async_computation.2 | async-start | bytes 3686400 | tf_op jit(solution)/shard_map/reduce_scatter | solution.py:335
Sparse Core Ops, SparseCore 0:
  10.2 64.6 all-gather.4
  77.1 60.5 all-gather.6
  214.2 67.0 all-reduce.1
  285.1 75.9 reduce-scatter.4
  364.6 75.0 reduce-scatter.2

commit v2 on v1

--- a/solution.py
+++ b/solution.py
@@ -50,19 +50,241 @@
     return pl.ds(pl.multiple_of(index * LANES, LANES), LANES)
 
 
+class Links:
+    def __init__(self, group, group_count, across_count):
+        self.group = group
+        self.across_count = across_count
+        self.along_count = group_count // across_count
+        self.along = group // across_count
+        self.across = lax.rem(group, across_count)
+
+    def at(self, along, across):
+        return along * self.across_count + across
+
+    def beside(self, step):
+        return lax.rem(self.across + step, self.across_count)
+
+    def far_first(self, turn):
+        low_half = self.along < self.along_count // 2
+        return jnp.where(low_half, self.along_count - 1 - turn, turn)
+
+    def next(self, way):
+        if way == 0:
+            there = self.along + 1 < self.along_count
+            place = jnp.minimum(self.along + 1, self.along_count - 1)
+        else:
+            there = self.along > 0
+            place = jnp.maximum(self.along - 1, 0)
+        return there, self.at(place, self.across)
+
+
+def slab(ref, place, height):
+    return ref.at[pl.ds(pl.multiple_of(place * height, 16), height), :]
+
+
+def gather_copies(links, weights, recv, line, side):
+    def copy(which, along, source, send_sem, peer):
+        own, full = weights[which]
+        origin = links.at(along, links.across)
+        target = slab(full, origin, own.shape[0])
+        return pltpu.make_async_remote_copy(
+            src_ref=own if source else target, dst_ref=target,
+            send_sem=send_sem, recv_sem=recv.at[which, origin],
+            device_id={"dp": peer}, device_id_type=MESH,
+        )
+
+    def to_line(which, along, way, source=False):
+        return copy(which, along, source, line.at[which, way, along], links.next(way)[1])
+
+    def to_side(which, along, step, source=False):
+        peer = links.at(links.along, links.beside(step))
+        return copy(which, along, source, side.at[which, step - 1, along], peer)
+
+    def arrival(which, along, across):
+        own, full = weights[which]
+        origin = links.at(along, across)
+        target = slab(full, origin, own.shape[0])
+        return pltpu.make_async_remote_copy(
+            src_ref=own, dst_ref=target, send_sem=line.at[which, 0, 0],
+            recv_sem=recv.at[which, origin],
+            device_id={"dp": links.next(0)[1]}, device_id_type=MESH,
+        )
+
+    return to_line, to_side, arrival
+
+
+def origin_at(links, distance, way):
+    if way == 0:
+        return links.along >= distance, jnp.maximum(links.along - distance, 0)
+    last = links.along_count - 1
+    return links.along + distance <= last, jnp.minimum(links.along + distance, last)
+
+
+def gather(links, weights, recv, line, side):
+    to_line, to_side, arrival = gather_copies(links, weights, recv, line, side)
+    for which in range(2):
+        for way in range(2):
+            @pl.when(links.next(way)[0])
+            def _():
+                to_line(which, links.along, way, True).start()
+
+        for step in range(1, links.across_count):
+            to_side(which, links.along, step, True).start()
+    for which in range(2):
+        own, full = weights[which]
+        height = own.shape[0]
+        full[pl.ds(pl.multiple_of(links.group * height, 16), height), :] = own[...]
+    for distance in range(1, links.along_count):
+        for which in range(2):
+            for way in range(2):
+                present, along = origin_at(links, distance, way)
+
+                @pl.when(present)
+                def _():
+                    arrival(which, along, links.across).wait_recv()
+
+                    @pl.when(links.next(way)[0])
+                    def _():
+                        to_line(which, along, way).start()
+
+                    for step in range(1, links.across_count):
+                        to_side(which, along, step).start()
+
+    for which in range(2):
+        for along in range(links.along_count):
+            for step in range(1, links.across_count):
+                arrival(which, along, links.beside(step)).wait_recv()
+
+
+def wait_gather_sends(links, weights, recv, line, side):
+    to_line, to_side, _ = gather_copies(links, weights, recv, line, side)
+    for which in range(2):
+        for distance in range(links.along_count):
+            for way in range(2):
+                present, along = origin_at(links, distance, way)
+
+                @pl.when(present & links.next(way)[0])
+                def _():
+                    to_line(which, along, way).wait_send()
+
+        for along in range(links.along_count):
+            for step in range(1, links.across_count):
+                to_side(which, along, step).wait_send()
+
+
+class Scatter:
+    def __init__(self, links, sums, sides, lines, side_send, side_recv, line_send, line_recv):
+        self.links, self.sums, self.sides, self.lines = links, sums, sides, lines
+        self.side_send, self.side_recv = side_send, side_recv
+        self.line_send, self.line_recv = line_send, line_recv
+
+    def side_copy(self, which, step, along):
+        links, buffer = self.links, self.sides[which]
+        peer = links.at(links.along, links.beside(step))
+        source = slab(self.sums[which], links.at(along, links.beside(step)), buffer.shape[2])
+        return pltpu.make_async_remote_copy(
+            src_ref=source, dst_ref=buffer.at[step - 1, along],
+            send_sem=self.side_send.at[which, step - 1, along],
+            recv_sem=self.side_recv.at[which, step - 1, along],
+            device_id={"dp": peer}, device_id_type=MESH,
+        )
+
+    def line_copy(self, which, way, along):
+        links, buffer = self.links, self.lines[which]
+        source = slab(self.sums[which], links.at(along, links.across), buffer.shape[2])
+        return pltpu.make_async_remote_copy(
+            src_ref=source, dst_ref=buffer.at[way, along],
+            send_sem=self.line_send.at[which, way, along],
+            recv_sem=self.line_recv.at[which, way, along],
+            device_id={"dp": links.next(way)[1]}, device_id_type=MESH,
+        )
+
+    def start_side(self, which, along):
+        for step in range(1, self.links.across_count):
+            self.side_copy(which, step, along).start()
+
+    def own_rows(self, which, along):
+        height = self.sides[which].shape[2]
+        place = self.links.at(along, self.links.across)
+        return pl.ds(pl.multiple_of(place * height, 16), height)
+
+    def across_sum(self, which, along):
+        total = self.sums[which][self.own_rows(which, along), :].astype(jnp.float32)
+        for step in range(1, self.links.across_count):
+            self.side_copy(which, step, along).wait_recv()
+            total = total + self.sides[which][step - 1, along].astype(jnp.float32)
+        return total
+
+    def pass_on(self, distance):
+        links = self.links
+        last = links.along_count - 1
+        for which in (1, 0):
+            for way in range(2):
+                if way == 0:
+                    present = links.along + distance <= last
+                    along = jnp.minimum(links.along + distance, last)
+                    behind = links.along > 0
+                else:
+                    present = links.along >= distance
+                    along = jnp.maximum(links.along - distance, 0)
+                    behind = links.along < last
+
+                @pl.when(present)
+                def _():
+                    rows = self.own_rows(which, along)
+                    self.sums[which][rows, :] = self.across_sum(which, along).astype(jnp.bfloat16)
+
+                    @pl.when(behind)
+                    def _():
+                        self.line_copy(which, way, along).wait_recv()
+                        more = self.lines[which][way, along].astype(jnp.float32)
+                        total = self.sums[which][rows, :].astype(jnp.float32) + more
+                        self.sums[which][rows, :] = total.astype(jnp.bfloat16)
+
+                    self.line_copy(which, way, along).start()
+
+    def finish(self, outputs):
+        links = self.links
+        for which in (1, 0):
+            outputs[which][...] = self.across_sum(which, links.along)
+            for way in range(2):
+                behind = links.along > 0 if way == 0 else links.along < links.along_count - 1
+
+                @pl.when(behind)
+                def _():
+                    self.line_copy(which, way, links.along).wait_recv()
+                    outputs[which][...] += self.lines[which][way, links.along].astype(jnp.float32)
+
+    def wait_sends(self):
+        links = self.links
+        for which in range(2):
+            for along in range(links.along_count):
+                for step in range(1, links.across_count):
+                    self.side_copy(which, step, along).wait_send()
+
+                @pl.when(along > links.along)
+                def _():
+                    self.line_copy(which, 0, along).wait_send()
+
+                @pl.when(along < links.along)
+                def _():
+                    self.line_copy(which, 1, along).wait_send()
+
+
 def kernel(
-    section_count, micro_count, slots,
-    x_ref, target_ref, live_ref, taps_ref, first_ref, second_ref, head_ref,
+    section_count, group_count, across_count, micro_count, slots, inside,
+    x_ref, target_ref, live_ref, taps_ref, own_first, own_second, head_ref,
     grad_in_ref, grad_out_ref, small_ref,
     tiles, results, ups, tile_grads, mixed, normed, normed_low, inverse, activated, slope,
     hidden_grad, kernel_acc, head_block,
     tile_send, tile_recv, up_send, up_recv, head_send, head_recv,
+    *more,
 ):
     section = lax.axis_index("section")
     last = section_count - 1
     cells = slots * SIDE * SIDE
     width = x_ref.shape[-1]
-    expand = first_ref.shape[1]
+    expand = own_first.shape[1]
     lane_tiles = width // LANES
     is_first = section == 0
     is_last = section == last
@@ -73,7 +295,24 @@
     for step in range(1, section_count):
         peer = lax.rem(section + step, section_count)
         pl.semaphore_signal(barrier, inc=1, device_id={"section": peer}, device_id_type=MESH)
-    pl.semaphore_wait(barrier, section_count - 1)
+    if inside:
+        group = lax.axis_index("dp")
+        for step in range(1, group_count):
+            peer = lax.rem(group + step, group_count)
+            pl.semaphore_signal(barrier, inc=1, device_id={"dp": peer}, device_id_type=MESH)
+    pl.semaphore_wait(barrier, section_count - 1 + (group_count - 1 if inside else 0))
+
+    if inside:
+        (
+            first_ref, second_ref, sum_in, sum_out, side_in, side_out, line_in, line_out,
+            stage, landed, gather_recv, gather_line, gather_side,
+            side_send, side_recv, line_send, line_recv, small_send, small_recv,
+        ) = more
+        links = Links(group, group_count, across_count)
+        weights = ((own_first, first_ref), (own_second, second_ref))
+        gather(links, weights, gather_recv, gather_line, gather_side)
+    else:
+        first_ref, second_ref, sum_in, sum_out = own_first, own_second, grad_in_ref, grad_out_ref
 
     def rows_of(micro):
         return pl.ds(pl.multiple_of(micro * cells, cells), cells)
@@ -219,18 +458,36 @@
     lax.fori_loop(0, micro_count, backward, 0)
 
     upstreams = ups[...].reshape(micro_count * cells, width)
-    for start in range(0, expand, CHUNK):
-        columns = slice(start, start + CHUNK)
-        grad_out_ref[columns, :] = lax.dot_general(
+    parts = expand // LANES // lane_tiles
+    if inside:
+        parts = links.along_count
+        scatter = Scatter(
+            links, (sum_in, sum_out), (side_in, side_out), (line_in, line_out),
+            side_send, side_recv, line_send, line_recv,
+        )
+    step_columns = expand // parts
+
+    def out_part(turn, carry):
+        part = links.far_first(turn) if inside else turn
+        columns = pl.ds(pl.multiple_of(part * step_columns, LANES), step_columns)
+        sum_out[columns, :] = lax.dot_general(
             activated[:, columns], upstreams, (((0,), (0,)), ((), ())),
             preferred_element_type=jnp.float32,
         ).astype(jnp.bfloat16)
+        if inside:
+            scatter.start_side(1, part)
+        return carry
+
+    lax.fori_loop(0, parts, out_part, 0)
     for start in range(0, expand, CHUNK):
         columns = slice(start, start + CHUNK)
-        grad_in_ref[:, columns] = lax.dot_general(
+        sum_in[:, columns] = lax.dot_general(
             normed_low[...], hidden_grad[:, columns], (((0,), (0,)), ((), ())),
             preferred_element_type=jnp.float32,
         ).astype(jnp.bfloat16)
+    if inside:
+        for turn in range(parts):
+            scatter.start_side(0, links.far_first(turn))
 
     kernel_acc[...] = jnp.zeros_like(kernel_acc)
 
@@ -250,7 +507,8 @@
         return carry
 
     lax.fori_loop(0, micro_count * lane_tiles, tap_grads, 0)
-    small_ref[0:HEAD_ROW, :] = jnp.sum(kernel_acc[...], axis=1)
+    small = stage.at[0] if inside else small_ref
+    small[0:HEAD_ROW, :] = jnp.sum(kernel_acc[...], axis=1)
 
     @pl.when(is_last)
     def _():
@@ -261,7 +519,38 @@
     def _():
         head_copy(1).wait_recv()
 
-    small_ref[HEAD_ROW:SMALL_ROWS, :] = head_block[...]
+    small[HEAD_ROW:SMALL_ROWS, :] = head_block[...]
+    if inside:
+        rounds = stage.shape[0] - 1
+
+        def small_copy(turn):
+            weight = 1 << turn
+            bit = lax.rem(group // weight, 2)
+            return pltpu.make_async_remote_copy(
+                src_ref=stage.at[turn], dst_ref=landed.at[turn],
+                send_sem=small_send.at[turn], recv_sem=small_recv.at[turn],
+                device_id={"dp": group + weight * (1 - 2 * bit)}, device_id_type=MESH,
+            )
+
+        def small_round(turn):
+            if turn < rounds:
+                small_copy(turn).wait()
+                stage[turn + 1] = stage[turn] + landed[turn]
+                if turn + 1 < rounds:
+                    small_copy(turn + 1).start()
+
+        small_copy(0).start()
+        level = 0
+        for distance in range(links.along_count - 1, 0, -1):
+            scatter.pass_on(distance)
+            small_round(level)
+            level += 1
+        scatter.finish((grad_in_ref, grad_out_ref))
+        for turn in range(level, rounds):
+            small_round(turn)
+        small_ref[...] = stage[rounds]
+        scatter.wait_sends()
+        wait_gather_sends(links, weights, gather_recv, gather_line, gather_side)
 
     def finish(micro, carry):
         @pl.when(jnp.logical_not(is_last))
@@ -290,58 +579,102 @@
     weights = jnp.broadcast_to(
         live[:, :, None].astype(jnp.float32), (micro_count, slots, SIDE * SIDE)
     ).reshape(micro_count, cells, 1)
-    first_full = lax.all_gather(weight_in[0], "dp", axis=0, tiled=True)
-    second_full = lax.all_gather(weight_out[0], "dp", axis=0, tiled=True)
+    group_count = lax.axis_size("dp")
+    height_in, height_out = weight_in.shape[1], weight_out.shape[1]
+    across_count = 1
+    while 4 * across_count * across_count <= group_count:
+        across_count *= 2
+    along_count = group_count // across_count
+    rounds = group_count.bit_length() - 1
+    inside = (
+        height_in % 16 == 0
+        and height_out % 16 == 0
+        and group_count == 1 << rounds
+        and group_count > 1
+        and across_count * height_out % LANES == 0
+    )
+    first, second = weight_in[0], weight_out[0]
+    if not inside:
+        first = lax.all_gather(first, "dp", axis=0, tiled=True)
+        second = lax.all_gather(second, "dp", axis=0, tiled=True)
     low, full = jnp.bfloat16, jnp.float32
     every = micro_count * cells
     in_vmem = pl.BlockSpec(memory_space=pltpu.VMEM)
+    shapes = [
+        ((height_in, expand), full) if inside else ((width, expand), low),
+        ((height_out, width), full) if inside else ((expand, width), low),
+        ((SMALL_ROWS, width), full),
+    ]
+    scratch = [
+        pltpu.VMEM((micro_count, cells, width), low),
+        pltpu.VMEM((micro_count, cells, width), low),
+        pltpu.VMEM((micro_count, cells, width), low),
+        pltpu.VMEM((micro_count, cells, width), low),
+        pltpu.VMEM((cells, width), full),
+        pltpu.VMEM((every, width), full),
+        pltpu.VMEM((every, width), low),
+        pltpu.VMEM((every, LANES), full),
+        pltpu.VMEM((every, expand), low),
+        pltpu.VMEM((every, expand), full),
+        pltpu.VMEM((every, expand), low),
+        pltpu.VMEM((HEAD_ROW, SIDE, width), full),
+        pltpu.VMEM((SMALL_ROWS - HEAD_ROW, width), full),
+        pltpu.SemaphoreType.DMA((micro_count,)),
+        pltpu.SemaphoreType.DMA((micro_count,)),
+        pltpu.SemaphoreType.DMA((micro_count,)),
+        pltpu.SemaphoreType.DMA((micro_count,)),
+        pltpu.SemaphoreType.DMA((section_count - 1,)),
+        pltpu.SemaphoreType.DMA,
+    ]
+    if inside:
+        sides = across_count - 1
+        scratch += [
+            pltpu.VMEM((width, expand), low),
+            pltpu.VMEM((expand, width), low),
+            pltpu.VMEM((width, expand), low),
+            pltpu.VMEM((expand, width), low),
+            pltpu.VMEM((sides, along_count, height_in, expand), low),
+            pltpu.VMEM((sides, along_count, height_out, width), low),
+            pltpu.VMEM((2, along_count, height_in, expand), low),
+            pltpu.VMEM((2, along_count, height_out, width), low),
+            pltpu.VMEM((rounds + 1, SMALL_ROWS, width), full),
+            pltpu.VMEM((rounds, SMALL_ROWS, width), full),
+            pltpu.SemaphoreType.DMA((2, group_count)),
+            pltpu.SemaphoreType.DMA((2, 2, along_count)),
+            pltpu.SemaphoreType.DMA((2, sides, along_count)),
+            pltpu.SemaphoreType.DMA((2, sides, along_count)),
+            pltpu.SemaphoreType.DMA((2, sides, along_count)),
+            pltpu.SemaphoreType.DMA((2, 2, along_count)),
+            pltpu.SemaphoreType.DMA((2, 2, along_count)),
+            pltpu.SemaphoreType.DMA((rounds,)),
+            pltpu.SemaphoreType.DMA((rounds,)),
+        ]
     grad_in, grad_out, small = pl.pallas_call(
-        functools.partial(kernel, section_count, micro_count, slots),
-        out_shape=(
-            jax.ShapeDtypeStruct((width, expand), low),
-            jax.ShapeDtypeStruct((expand, width), low),
-            jax.ShapeDtypeStruct((SMALL_ROWS, width), full),
+        functools.partial(
+            kernel, section_count, group_count, across_count, micro_count, slots, inside
         ),
+        out_shape=tuple(jax.ShapeDtypeStruct(shape, kind) for shape, kind in shapes),
         in_specs=[in_vmem] * 7,
         out_specs=(in_vmem,) * 3,
-        scratch_shapes=[
-            pltpu.VMEM((micro_count, cells, width), low),
-            pltpu.VMEM((micro_count, cells, width), low),
-            pltpu.VMEM((micro_count, cells, width), low),
-            pltpu.VMEM((micro_count, cells, width), low),
-            pltpu.VMEM((cells, width), full),
-            pltpu.VMEM((every, width), full),
-            pltpu.VMEM((every, width), low),
-            pltpu.VMEM((every, LANES), full),
-            pltpu.VMEM((every, expand), low),
-            pltpu.VMEM((every, expand), full),
-            pltpu.VMEM((every, expand), low),
-            pltpu.VMEM((HEAD_ROW, SIDE, width), full),
-            pltpu.VMEM((SMALL_ROWS - HEAD_ROW, width), full),
-            pltpu.SemaphoreType.DMA((micro_count,)),
-            pltpu.SemaphoreType.DMA((micro_count,)),
-            pltpu.SemaphoreType.DMA((micro_count,)),
-            pltpu.SemaphoreType.DMA((micro_count,)),
-            pltpu.SemaphoreType.DMA((section_count - 1,)),
-            pltpu.SemaphoreType.DMA,
-        ],
+        scratch_shapes=scratch,
         compiler_params=pltpu.CompilerParams(
-            collective_id=0, has_side_effects=True, vmem_limit_bytes=56 * 1024 * 1024
+            collective_id=0, has_side_effects=True, vmem_limit_bytes=60 * 1024 * 1024
         ),
         cost_estimate=pl.CostEstimate(
             flops=12 * every * width * expand, bytes_accessed=8 * width * expand, transcendentals=0
         ),
-    )(entering, targets, weights, depth_kernels[0], first_full, second_full, head_weight[None])
-    grad_in_part = lax.psum_scatter(grad_in, "dp", scatter_dimension=0, tiled=True)
-    grad_out_part = lax.psum_scatter(grad_out, "dp", scatter_dimension=0, tiled=True)
-    small_total = lax.psum(small, "dp")
+    )(entering, targets, weights, depth_kernels[0], first, second, head_weight[None])
+    if not inside:
+        grad_in = lax.psum_scatter(grad_in, "dp", scatter_dimension=0, tiled=True).astype(full)
+        grad_out = lax.psum_scatter(grad_out, "dp", scatter_dimension=0, tiled=True).astype(full)
+        small = lax.psum(small, "dp")
     taps = depth_kernels.shape[1]
     return (
-        grad_in_part.astype(full)[None],
-        grad_out_part.astype(full)[None],
-        small_total[:taps][None],
-        small_total[HEAD_ROW],
-        small_total[HEAD_ROW + 1, 0],
+        grad_in[None],
+        grad_out[None],
+        small[:taps][None],
+        small[HEAD_ROW],
+        small[HEAD_ROW + 1, 0],
     )
 
 

time: 449 us -> 268 us (0.60)
  waiting for transfers between devices: 341 us -> 0 us
  Pallas kernels: 76.4 us -> 253 us
  between operations: 13.8 us -> 0.67 us
  other arithmetic: 7.46 us -> 2.47 us
    pallas_call x1, Pallas kernels: 76.4 us -> 253 us  [body(): pl.pallas_call(functools.partial(kernel, section_count, group_count, acro...]
    reduce_scatter x2 -> x0, waiting for transfers between devices: 152 us -> none  [the longest x1 76.6 us: body(): lax.psum_scatter(grad_in, 'dp', scatter_dimension=0, tiled=True)]
    all_gather x2 -> x0, waiting for transfers between devices: 121 us -> none  [the longest x1 62.8 us: body(): second_full = lax.all_gather(weight_out[0], 'dp', axis=0, tiled=True)]
    psum x1 -> x0, waiting for transfers between devices: 66 us -> none  [body(): small_total = lax.psum(small, 'dp')]
  transfers between devices with their start and end apart: 5 -> 0, of which waited for: 5 -> 0; matrix products, arithmetic and copies ran while one was open for 3% -> 0% of each run, Pallas kernels for 0% -> 0%
where the time goes in v2:
time: 268 us
  Pallas kernels  253 us (94%)
  local copies, waits for them, and re-layouts  11.3 us (4%)
    pallas_call x1, Pallas kernels, body(): pl.pallas_call(functools.partial(kernel, section_count, group_count, acro...  253 us

profile of v2, /device:TPU:0, one launch (start us, length us, event | category | flops | bytes accessed | tf_op | source)
XLA Modules:
  0.0 267.6 jit_solution(876534050267471731)
XLA Ops:
  0.6 0.0 copy-start.2
  0.6 0.0 copy-start.1
  0.7 1.3 broadcast_in_dim.21.head_ref
  2.0 0.7 fusion
  2.7 0.1 broadcast_in_dim.20
  2.8 0.1 mul.13
  2.9 0.1 mul.14
  3.0 0.8 convert_element_type.22
  3.7 0.0 copy-done.2
  3.7 0.7 copy.18
  4.4 0.8 convert_element_type.25.target_ref
  5.2 0.9 reshape.81.live_ref
  6.1 0.0 copy-done.1
  6.1 1.0 broadcast_multiply_fusion.x_ref
  7.1 253.2 %shard_map.110 = (f32[80,2560]{1,0:T(8,128)}, f32[320,640]{1,0:T(8,128)}, f32[64,640]{1,0:T(8,128)}) custom-call(bf16[4,128,640]{2,1,0:T(8,128)(2,1)} %broadcast_multiply_fusion.x_ref, f32[4,128,1]{2,1,0:T(8,128)} %convert_element_type.25.target_ref, f32[4,128,1]{2,1,0:T(8,128)} %reshape.81.live_ref, f32[49,640]{1,0:T(8,128)} %bitcast.19, ...), custom_call_target="tpu_custom_call" | custom-call | flops 10066329600 | bytes 13107200 | tf_op jit(solution)/shard_map/pallas_call | solution.py:652
  260.3 1.2 slice.11
  261.5 1.3 slice_reduce_fusion
  262.8 0.9 slice_bitcast_fusion
  263.8 0.8 copy.15
  264.6 0.0 copy-start
  264.6 2.2 copy.21
  266.7 0.0 copy-done
  266.7 0.9 copy.22
Async XLA Ops:
  0.6 3.1 %copy-start.2 = (f32[1,49,640]{2,0,1:T(1,128)S(1)}, f32[1,49,640]{2,0,1:T(1,128)}, u32[]{:S(2)}) copy-start(f32[1,49,640]{2,0,1:T(1,128)} %param.10) | copy-start | bytes 376324
  0.6 5.5 %copy-start.1 = (bf16[1,4,2,8,8,640]{5,4,3,2,1,0:T(8,128)(2,1)S(1)}, bf16[1,4,2,8,8,640]{5,4,3,2,1,0:T(8,128)(2,1)}, u32[]{:S(2)}) copy-start(bf16[1,4,2,8,8,640]{5,4,3,2,1,0:T(8,128)(2,1)} %param.7) | copy-start | bytes 1966084
  264.6 2.2 copy-start

commit v3 on v1

--- a/solution.py
+++ b/solution.py
@@ -50,30 +50,404 @@
     return pl.ds(pl.multiple_of(index * LANES, LANES), LANES)
 
 
+class Place:
+    def __init__(self):
+        group, self.home = lax.axis_index("dp"), lax.axis_index("section")
+        self.group = group
+        self.along, self.across = group // 2, lax.rem(group, 2)
+        self.row, self.core = self.home // 2, lax.rem(self.home, 2)
+        self.role = self.swap(self.along)
+        self.role_row, self.role_core = lax.rem(self.along, 2), self.along // 2
+        self.keeper = self.home == self.role
+
+    def swap(self, index):
+        return 2 * lax.rem(index, 2) + index // 2
+
+    def at(self, along=None, across=None, row=None, core=None):
+        along = self.along if along is None else along
+        across = self.across if across is None else across
+        row = self.row if row is None else row
+        core = self.core if core is None else core
+        return {"dp": 2 * along + across, "section": 2 * row + core}
+
+    def near_first(self, turn):
+        return jnp.where(
+            self.along < 2, lax.rem(self.along + turn, 4), lax.rem(self.along - turn + 4, 4)
+        )
+
+    def far_first(self, turn):
+        return jnp.where(self.along < 2, 3 - turn, turn)
+
+
+def remote(source, target, send_sem, recv_sem, device):
+    return pltpu.make_async_remote_copy(
+        src_ref=source, dst_ref=target, send_sem=send_sem, recv_sem=recv_sem,
+        device_id=device, device_id_type=MESH,
+    )
+
+
+def slab(ref, place, height):
+    return ref.at[pl.ds(pl.multiple_of(place * height, 16), height), :]
+
+
+class Gather:
+    def __init__(self, place, weights, recv, first_send, core_send, across_send, row_send):
+        self.place, self.weights, self.recv = place, weights, recv
+        self.first_send, self.core_send = first_send, core_send
+        self.across_send, self.row_send = across_send, row_send
+
+    def shard(self, which, origin):
+        own, full = self.weights[which]
+        return slab(full, origin, own.shape[0])
+
+    def launch(self, which):
+        place = self.place
+        plane = place.swap(place.home)
+        target = self.shard(which, place.group)
+        return remote(
+            self.weights[which][0], target, self.first_send.at[which],
+            self.recv.at[which, place.group], place.at(along=plane, core=which),
+        )
+
+    def stays(self, which):
+        return self.place.keeper & (self.place.core == which)
+
+    def spread(self, which, origin, sem, device):
+        target = self.shard(which, origin)
+        return remote(target, target, sem, self.recv.at[which, origin], device)
+
+    def to_core(self, which, origin):
+        place = self.place
+        return self.spread(
+            which, origin, self.core_send.at[origin], place.at(core=1 - place.core)
+        )
+
+    def to_across(self, which, along):
+        place = self.place
+        return self.spread(
+            which, 2 * along + place.across, self.across_send.at[along],
+            place.at(across=1 - place.across),
+        )
+
+    def to_row(self, which, along):
+        place = self.place
+        return self.spread(
+            which, 2 * along + place.across, self.row_send.at[along], place.at(row=1 - place.row)
+        )
+
+    def start(self):
+        for which in range(2):
+            stays = self.stays(which)
+
+            @pl.when(jnp.logical_not(stays))
+            def _():
+                self.launch(which).start()
+
+            @pl.when(stays)
+            def _():
+                own, full = self.weights[which]
+                height = own.shape[0]
+                start = pl.multiple_of(self.place.group * height, 16)
+                full[pl.ds(start, height), :] = own[...]
+
+    def run(self):
+        place = self.place
+        in_row = place.row == place.role_row
+        for which in range(2):
+
+            @pl.when(place.core == which)
+            def _():
+                for turn in range(4):
+                    along = place.near_first(turn)
+                    origin = 2 * along + place.across
+                    if turn == 0:
+
+                        @pl.when(jnp.logical_not(place.keeper))
+                        def _():
+                            self.to_core(which, origin).wait_recv()
+                    else:
+                        self.to_core(which, origin).wait_recv()
+                    self.to_across(which, along).start()
+
+                    @pl.when(in_row)
+                    def _():
+                        self.to_row(which, along).start()
+
+                    self.to_core(which, origin).start()
+                for turn in range(4):
+                    origin = 2 * place.near_first(turn) + 1 - place.across
+                    self.to_core(which, origin).wait_recv()
+                    self.to_core(which, origin).start()
+
+        for which in range(2):
+
+            @pl.when(place.core != which)
+            def _():
+                for origin in range(8):
+                    self.to_core(which, origin).wait_recv()
+
+    def wait_sends(self):
+        place = self.place
+        for which in range(2):
+
+            @pl.when(jnp.logical_not(self.stays(which)))
+            def _():
+                self.launch(which).wait_send()
+
+            @pl.when(place.core == which)
+            def _():
+                for along in range(4):
+                    self.to_across(which, along).wait_send()
+
+                    @pl.when(place.row == place.role_row)
+                    def _():
+                        self.to_row(which, along).wait_send()
+
+                for origin in range(8):
+                    self.to_core(which, origin).wait_send()
+
+
+class Scatter:
+    def __init__(self, place, sums, cores, sides, rows, homes, sems):
+        self.place, self.sums, self.cores = place, sums, cores
+        self.sides, self.rows, self.homes = sides, rows, homes
+        (
+            self.core_send, self.core_recv, self.side_send, self.side_recv,
+            self.row_send, self.row_recv, self.home_send, self.home_recv,
+        ) = sems
+
+    def height(self, which):
+        return self.sides[which].shape[1]
+
+    def core_copy(self, which, along):
+        place, height = self.place, 2 * self.height(which)
+        return remote(
+            slab(self.sums[which], along, height), slab(self.cores[which], along, height),
+            self.core_send.at[along], self.core_recv.at[along], place.at(core=1 - place.core),
+        )
+
+    def side_copy(self, which, along):
+        place = self.place
+        source = slab(self.sums[which], 2 * along + 1 - place.across, self.height(which))
+        return remote(
+            source, self.sides[which].at[along], self.side_send.at[along],
+            self.side_recv.at[along], place.at(across=1 - place.across),
+        )
+
+    def row_copy(self, which, along):
+        place = self.place
+        source = slab(self.sums[which], 2 * along + place.across, self.height(which))
+        return remote(
+            source, self.rows[which].at[along], self.row_send.at[along],
+            self.row_recv.at[along], place.at(row=1 - place.row),
+        )
+
+    def home_copy(self, which, along):
+        place = self.place
+        source = slab(self.sums[which], 2 * along + place.across, self.height(which))
+        return remote(
+            source, self.homes[which], self.home_send.at[along], self.home_recv.at[which],
+            place.at(along=along, core=place.role_core),
+        )
+
+    def goes(self, along):
+        place = self.place
+        return (along != place.along) | (place.core != place.role_core)
+
+    def add(self, which, along, count, first, buffer):
+        height = count * self.height(which)
+        start = pl.multiple_of(first * self.height(which), 16)
+        rows = pl.ds(start, height)
+        total = self.sums[which][rows, :].astype(jnp.float32) + buffer.astype(jnp.float32)
+        self.sums[which][rows, :] = total.astype(jnp.bfloat16)
+
+    def give_core(self, which, along):
+        @pl.when(self.place.core != which)
+        def _():
+            self.core_copy(which, along).start()
+
+    def over_core(self, turn):
+        along = self.place.far_first(turn)
+        for which in range(2):
+
+            @pl.when(self.place.core == which)
+            def _():
+                self.core_copy(which, along).wait_recv()
+                height = 2 * self.height(which)
+                start = pl.multiple_of(along * height, 16)
+                self.add(which, along, 2, 2 * along, self.cores[which][pl.ds(start, height), :])
+                self.side_copy(which, along).start()
+
+    def over_plane(self, turn):
+        place = self.place
+        along = place.far_first(turn)
+        in_row = place.row == place.role_row
+        for which in range(2):
+
+            @pl.when(place.core == which)
+            def _():
+                self.side_copy(which, along).wait_recv()
+                own = 2 * along + place.across
+                self.add(which, along, 1, own, self.sides[which][along])
+
+                @pl.when(jnp.logical_not(in_row))
+                def _():
+                    self.row_copy(which, along).start()
+
+                @pl.when(in_row)
+                def _():
+                    self.row_copy(which, along).wait_recv()
+                    self.add(which, along, 1, own, self.rows[which][along])
+
+                    @pl.when(self.goes(along))
+                    def _():
+                        self.home_copy(which, along).start()
+
+                    @pl.when(jnp.logical_not(self.goes(along)))
+                    def _():
+                        height = self.height(which)
+                        start = pl.multiple_of(own * height, 16)
+                        self.homes[which][...] = self.sums[which][pl.ds(start, height), :]
+
+    def finish(self, outputs):
+        place = self.place
+        for which in range(2):
+            here = place.keeper & (place.core == which)
+
+            @pl.when(jnp.logical_not(here))
+            def _():
+                self.home_copy(which, 0).wait_recv()
+
+            outputs[which][...] = self.homes[which][...].astype(jnp.float32)
+
+    def wait_sends(self):
+        place = self.place
+        in_row = place.row == place.role_row
+        for which in range(2):
+            for along in range(4):
+
+                @pl.when(place.core != which)
+                def _():
+                    self.core_copy(which, along).wait_send()
+
+                @pl.when(place.core == which)
+                def _():
+                    self.side_copy(which, along).wait_send()
+
+                    @pl.when(jnp.logical_not(in_row))
+                    def _():
+                        self.row_copy(which, along).wait_send()
+
+                    @pl.when(in_row & self.goes(along))
+                    def _():
+                        self.home_copy(which, along).wait_send()
+
+
 def kernel(
-    section_count, micro_count, slots,
-    x_ref, target_ref, live_ref, taps_ref, first_ref, second_ref, head_ref,
+    section_count, micro_count, slots, inside,
+    x_ref, own_labels, own_taps, own_first, own_second, head_ref,
     grad_in_ref, grad_out_ref, small_ref,
     tiles, results, ups, tile_grads, mixed, normed, normed_low, inverse, activated, slope,
     hidden_grad, kernel_acc, head_block,
     tile_send, tile_recv, up_send, up_recv, head_send, head_recv,
+    *more,
 ):
-    section = lax.axis_index("section")
     last = section_count - 1
+    if inside:
+        place = Place()
+        section = place.role
+        peers = [place.at(along=lax.rem(place.along + step, 4)) for step in range(1, 4)]
+        peers += [
+            place.at(along=lax.rem(place.along + step, 4), core=1 - place.core)
+            for step in range(4)
+        ]
+        peers += [place.at(row=1 - place.row)]
+        peers += [place.at(row=1 - place.row, core=1 - place.core)]
+        peers += [place.at(across=1 - place.across)]
+    else:
+        section = lax.axis_index("section")
+        peers = [
+            {"section": lax.rem(section + step, section_count)} for step in range(1, section_count)
+        ]
     cells = slots * SIDE * SIDE
     width = x_ref.shape[-1]
-    expand = first_ref.shape[1]
+    expand = own_first.shape[1]
     lane_tiles = width // LANES
     is_first = section == 0
     is_last = section == last
     following = jnp.minimum(section + 1, last)
     previous = jnp.maximum(section - 1, 0)
 
+    def worker(index):
+        return place.at(along=place.swap(index)) if inside else {"section": index}
+
     barrier = pltpu.get_barrier_semaphore()
-    for step in range(1, section_count):
-        peer = lax.rem(section + step, section_count)
-        pl.semaphore_signal(barrier, inc=1, device_id={"section": peer}, device_id_type=MESH)
-    pl.semaphore_wait(barrier, section_count - 1)
+    for peer in peers:
+        pl.semaphore_signal(barrier, inc=1, device_id=peer, device_id_type=MESH)
+    pl.semaphore_wait(barrier, len(peers))
+
+    if inside:
+        (
+            first_ref, second_ref, sum_in, sum_out, core_in, core_out, side_in, side_out,
+            row_in, row_out, home_in, home_out, stage, landed, home_small, taps_ref, labels,
+            gather_recv, launch_send, spread_core, spread_across, spread_row,
+            core_send, core_recv, side_send, side_recv, row_send, row_recv, home_send, home_recv,
+            small_send, small_recv, back_send, back_recv, crop_send, label_send, label_recv,
+            taps_send, taps_recv,
+        ) = more
+        is_source = place.along == place.home
+
+        def crop_copy(micro):
+            return remote(
+                x_ref.at[micro], tiles.at[micro], crop_send.at[micro], tile_recv.at[micro],
+                place.at(along=0),
+            )
+
+        label_copy = remote(own_labels, labels, label_send, label_recv, place.at(along=3))
+
+        def taps_copy(step):
+            device = {"dp": place.group, "section": lax.rem(place.home + step, 4)}
+            return remote(own_taps, taps_ref, taps_send.at[step - 1], taps_recv, device)
+
+        gather = Gather(
+            place, ((own_first, first_ref), (own_second, second_ref)),
+            gather_recv, launch_send, spread_core, spread_across, spread_row,
+        )
+        gather.start()
+
+        @pl.when(place.keeper)
+        def _():
+            for step in range(1, 4):
+                taps_copy(step).start()
+            taps_ref[...] = own_taps[...]
+
+        @pl.when(is_source & (place.along != 0))
+        def _():
+            for micro in range(micro_count):
+                crop_copy(micro).start()
+
+        @pl.when(is_source & (place.along != 3))
+        def _():
+            label_copy.start()
+
+        @pl.when(is_source & (place.along == 3))
+        def _():
+            labels[...] = own_labels[...]
+
+        gather.run()
+
+        @pl.when(jnp.logical_not(place.keeper))
+        def _():
+            taps_copy(1).wait_recv()
+
+        @pl.when((place.along == 3) & jnp.logical_not(is_source))
+        def _():
+            label_copy.wait_recv()
+
+        own_crops = is_first & (place.home == 0)
+    else:
+        first_ref, second_ref, sum_in, sum_out = own_first, own_second, grad_in_ref, grad_out_ref
+        taps_ref, labels, own_crops = own_taps, own_labels, is_first
 
     def rows_of(micro):
         return pl.ds(pl.multiple_of(micro * cells, cells), cells)
@@ -82,14 +456,14 @@
         return pltpu.make_async_remote_copy(
             src_ref=results.at[micro], dst_ref=tiles.at[micro],
             send_sem=tile_send.at[micro], recv_sem=tile_recv.at[micro],
-            device_id={"section": following}, device_id_type=MESH,
+            device_id=worker(following), device_id_type=MESH,
         )
 
     def up_copy(micro):
         return pltpu.make_async_remote_copy(
             src_ref=tile_grads.at[micro], dst_ref=ups.at[micro],
             send_sem=up_send.at[micro], recv_sem=up_recv.at[micro],
-            device_id={"section": previous}, device_id_type=MESH,
+            device_id=worker(previous), device_id_type=MESH,
         )
 
     def head_copy(step):
@@ -97,7 +471,7 @@
         return pltpu.make_async_remote_copy(
             src_ref=head_block, dst_ref=head_block,
             send_sem=head_send.at[step - 1], recv_sem=head_recv,
-            device_id={"section": peer}, device_id_type=MESH,
+            device_id=worker(peer), device_id_type=MESH,
         )
 
     @pl.when(is_last)
@@ -105,11 +479,11 @@
         head_block[...] = jnp.zeros_like(head_block)
 
     def forward(micro, carry):
-        @pl.when(is_first)
+        @pl.when(own_crops)
         def _():
             tiles[micro] = x_ref[micro]
 
-        @pl.when(jnp.logical_not(is_first))
+        @pl.when(jnp.logical_not(own_crops))
         def _():
             tile_copy(micro).wait_recv()
 
@@ -153,8 +527,8 @@
         def _():
             final = results[micro].astype(jnp.float32)
             logits = jnp.sum(final * head_ref[...], axis=-1, keepdims=True)
-            weight = live_ref[micro]
-            truth = target_ref[micro]
+            truth = labels[micro, :, 0:1]
+            weight = labels[micro, :, 1:2]
             factor = 1.0 / (micro_count * slots)
             softplus = jnp.maximum(logits, 0.0) + jnp.log1p(jnp.exp(-jnp.abs(logits)))
             loss = jnp.sum(weight * (softplus - truth * logits)) * factor
@@ -219,18 +593,42 @@
     lax.fori_loop(0, micro_count, backward, 0)
 
     upstreams = ups[...].reshape(micro_count * cells, width)
-    for start in range(0, expand, CHUNK):
-        columns = slice(start, start + CHUNK)
-        grad_out_ref[columns, :] = lax.dot_general(
+    parts = expand // LANES // lane_tiles
+    if inside:
+        parts = 4
+        scatter = Scatter(
+            place, (sum_in, sum_out), (core_in, core_out), (side_in, side_out),
+            (row_in, row_out), (home_in, home_out),
+            (
+                core_send, core_recv, side_send, side_recv,
+                row_send, row_recv, home_send, home_recv,
+            ),
+        )
+    step_columns = expand // parts
+
+    def out_part(turn, carry):
+        part = place.far_first(turn) if inside else turn
+        columns = pl.ds(pl.multiple_of(part * step_columns, LANES), step_columns)
+        sum_out[columns, :] = lax.dot_general(
             activated[:, columns], upstreams, (((0,), (0,)), ((), ())),
             preferred_element_type=jnp.float32,
         ).astype(jnp.bfloat16)
+        if inside:
+            scatter.give_core(1, part)
+        return carry
+
+    lax.fori_loop(0, parts, out_part, 0)
     for start in range(0, expand, CHUNK):
         columns = slice(start, start + CHUNK)
-        grad_in_ref[:, columns] = lax.dot_general(
+        sum_in[:, columns] = lax.dot_general(
             normed_low[...], hidden_grad[:, columns], (((0,), (0,)), ((), ())),
             preferred_element_type=jnp.float32,
         ).astype(jnp.bfloat16)
+    if inside:
+        for turn in range(parts):
+            scatter.give_core(0, place.far_first(turn))
+        for turn in range(parts):
+            scatter.over_core(turn)
 
     kernel_acc[...] = jnp.zeros_like(kernel_acc)
 
@@ -250,7 +648,8 @@
         return carry
 
     lax.fori_loop(0, micro_count * lane_tiles, tap_grads, 0)
-    small_ref[0:HEAD_ROW, :] = jnp.sum(kernel_acc[...], axis=1)
+    small = stage.at[0] if inside else small_ref
+    small[0:HEAD_ROW, :] = jnp.sum(kernel_acc[...], axis=1)
 
     @pl.when(is_last)
     def _():
@@ -261,7 +660,65 @@
     def _():
         head_copy(1).wait_recv()
 
-    small_ref[HEAD_ROW:SMALL_ROWS, :] = head_block[...]
+    small[HEAD_ROW:SMALL_ROWS, :] = head_block[...]
+    if inside:
+        partners = (
+            place.at(core=1 - place.core),
+            place.at(across=1 - place.across),
+            place.at(row=1 - place.row),
+        )
+
+        def small_copy(turn):
+            return remote(
+                stage.at[turn], landed.at[turn], small_send.at[turn], small_recv.at[turn],
+                partners[turn],
+            )
+
+        def back_copy(step):
+            return remote(
+                stage.at[3], home_small, back_send.at[step - 1], back_recv,
+                place.at(along=lax.rem(place.along + step, 4)),
+            )
+
+        small_copy(0).start()
+        for turn in range(parts):
+            scatter.over_plane(turn)
+            if turn < 3:
+                small_copy(turn).wait()
+                stage[turn + 1] = stage[turn] + landed[turn]
+                if turn < 2:
+                    small_copy(turn + 1).start()
+                else:
+
+                    @pl.when(place.keeper)
+                    def _():
+                        for step in range(1, 4):
+                            back_copy(step).start()
+                        home_small[...] = stage[3]
+
+        @pl.when(jnp.logical_not(place.keeper))
+        def _():
+            back_copy(1).wait_recv()
+
+        small_ref[...] = home_small[...]
+        scatter.finish((grad_in_ref, grad_out_ref))
+        scatter.wait_sends()
+        gather.wait_sends()
+
+        @pl.when(place.keeper)
+        def _():
+            for step in range(1, 4):
+                back_copy(step).wait_send()
+                taps_copy(step).wait_send()
+
+        @pl.when(is_source & (place.along != 0))
+        def _():
+            for micro in range(micro_count):
+                crop_copy(micro).wait_send()
+
+        @pl.when(is_source & (place.along != 3))
+        def _():
+            label_copy.wait_send()
 
     def finish(micro, carry):
         @pl.when(jnp.logical_not(is_last))
@@ -290,58 +747,96 @@
     weights = jnp.broadcast_to(
         live[:, :, None].astype(jnp.float32), (micro_count, slots, SIDE * SIDE)
     ).reshape(micro_count, cells, 1)
-    first_full = lax.all_gather(weight_in[0], "dp", axis=0, tiled=True)
-    second_full = lax.all_gather(weight_out[0], "dp", axis=0, tiled=True)
+    lane = jnp.arange(LANES)
+    labels = jnp.where(lane == 0, targets, 0.0) + jnp.where(lane == 1, weights, 0.0)
+    group_count = lax.axis_size("dp")
+    height_in, height_out = weight_in.shape[1], weight_out.shape[1]
+    inside = (
+        section_count == 4
+        and group_count == 8
+        and height_in % 16 == 0
+        and height_out % 16 == 0
+        and 2 * height_out % LANES == 0
+    )
+    first, second = weight_in[0], weight_out[0]
+    if not inside:
+        first = lax.all_gather(first, "dp", axis=0, tiled=True)
+        second = lax.all_gather(second, "dp", axis=0, tiled=True)
     low, full = jnp.bfloat16, jnp.float32
     every = micro_count * cells
     in_vmem = pl.BlockSpec(memory_space=pltpu.VMEM)
+    shapes = [
+        ((height_in, expand), full) if inside else ((width, expand), low),
+        ((height_out, width), full) if inside else ((expand, width), low),
+        ((SMALL_ROWS, width), full),
+    ]
+    scratch = [
+        pltpu.VMEM((micro_count, cells, width), low),
+        pltpu.VMEM((micro_count, cells, width), low),
+        pltpu.VMEM((micro_count, cells, width), low),
+        pltpu.VMEM((micro_count, cells, width), low),
+        pltpu.VMEM((cells, width), full),
+        pltpu.VMEM((every, width), full),
+        pltpu.VMEM((every, width), low),
+        pltpu.VMEM((every, LANES), full),
+        pltpu.VMEM((every, expand), low),
+        pltpu.VMEM((every, expand), full),
+        pltpu.VMEM((every, expand), low),
+        pltpu.VMEM((HEAD_ROW, SIDE, width), full),
+        pltpu.VMEM((SMALL_ROWS - HEAD_ROW, width), full),
+        pltpu.SemaphoreType.DMA((micro_count,)),
+        pltpu.SemaphoreType.DMA((micro_count,)),
+        pltpu.SemaphoreType.DMA((micro_count,)),
+        pltpu.SemaphoreType.DMA((micro_count,)),
+        pltpu.SemaphoreType.DMA((section_count - 1,)),
+        pltpu.SemaphoreType.DMA,
+    ]
+    if inside:
+        dma = pltpu.SemaphoreType.DMA
+        whole = [pltpu.VMEM((width, expand), low), pltpu.VMEM((expand, width), low)]
+        slabs = [
+            pltpu.VMEM((4, height_in, expand), low), pltpu.VMEM((4, height_out, width), low)
+        ]
+        scratch += whole * 3 + slabs * 2
+        scratch += [
+            pltpu.VMEM((height_in, expand), low),
+            pltpu.VMEM((height_out, width), low),
+            pltpu.VMEM((4, SMALL_ROWS, width), full),
+            pltpu.VMEM((3, SMALL_ROWS, width), full),
+            pltpu.VMEM((SMALL_ROWS, width), full),
+            pltpu.VMEM(depth_kernels.shape[1:], full),
+            pltpu.VMEM(labels.shape, full),
+            dma((2, 8)), dma((2,)), dma((8,)), dma((4,)), dma((4,)),
+            dma((4,)), dma((4,)), dma((4,)), dma((4,)), dma((4,)), dma((4,)), dma((4,)), dma((2,)),
+            dma((3,)), dma((3,)), dma((3,)), dma, dma((micro_count,)), dma, dma,
+            dma((3,)), dma,
+        ]
     grad_in, grad_out, small = pl.pallas_call(
-        functools.partial(kernel, section_count, micro_count, slots),
-        out_shape=(
-            jax.ShapeDtypeStruct((width, expand), low),
-            jax.ShapeDtypeStruct((expand, width), low),
-            jax.ShapeDtypeStruct((SMALL_ROWS, width), full),
+        functools.partial(
+            kernel, section_count, micro_count, slots, inside
         ),
-        in_specs=[in_vmem] * 7,
+        out_shape=tuple(jax.ShapeDtypeStruct(shape, kind) for shape, kind in shapes),
+        in_specs=[in_vmem] * 6,
         out_specs=(in_vmem,) * 3,
-        scratch_shapes=[
-            pltpu.VMEM((micro_count, cells, width), low),
-            pltpu.VMEM((micro_count, cells, width), low),
-            pltpu.VMEM((micro_count, cells, width), low),
-            pltpu.VMEM((micro_count, cells, width), low),
-            pltpu.VMEM((cells, width), full),
-            pltpu.VMEM((every, width), full),
-            pltpu.VMEM((every, width), low),
-            pltpu.VMEM((every, LANES), full),
-            pltpu.VMEM((every, expand), low),
-            pltpu.VMEM((every, expand), full),
-            pltpu.VMEM((every, expand), low),
-            pltpu.VMEM((HEAD_ROW, SIDE, width), full),
-            pltpu.VMEM((SMALL_ROWS - HEAD_ROW, width), full),
-            pltpu.SemaphoreType.DMA((micro_count,)),
-            pltpu.SemaphoreType.DMA((micro_count,)),
-            pltpu.SemaphoreType.DMA((micro_count,)),
-            pltpu.SemaphoreType.DMA((micro_count,)),
-            pltpu.SemaphoreType.DMA((section_count - 1,)),
-            pltpu.SemaphoreType.DMA,
-        ],
+        scratch_shapes=scratch,
         compiler_params=pltpu.CompilerParams(
-            collective_id=0, has_side_effects=True, vmem_limit_bytes=56 * 1024 * 1024
+            collective_id=0, has_side_effects=True, vmem_limit_bytes=60 * 1024 * 1024
         ),
         cost_estimate=pl.CostEstimate(
             flops=12 * every * width * expand, bytes_accessed=8 * width * expand, transcendentals=0
         ),
-    )(entering, targets, weights, depth_kernels[0], first_full, second_full, head_weight[None])
-    grad_in_part = lax.psum_scatter(grad_in, "dp", scatter_dimension=0, tiled=True)
-    grad_out_part = lax.psum_scatter(grad_out, "dp", scatter_dimension=0, tiled=True)
-    small_total = lax.psum(small, "dp")
+    )(entering, labels, depth_kernels[0], first, second, head_weight[None])
+    if not inside:
+        grad_in = lax.psum_scatter(grad_in, "dp", scatter_dimension=0, tiled=True).astype(full)
+        grad_out = lax.psum_scatter(grad_out, "dp", scatter_dimension=0, tiled=True).astype(full)
+        small = lax.psum(small, "dp")
     taps = depth_kernels.shape[1]
     return (
-        grad_in_part.astype(full)[None],
-        grad_out_part.astype(full)[None],
-        small_total[:taps][None],
-        small_total[HEAD_ROW],
-        small_total[HEAD_ROW + 1, 0],
+        grad_in[None],
+        grad_out[None],
+        small[:taps][None],
+        small[HEAD_ROW],
+        small[HEAD_ROW + 1, 0],
     )
 
 

time: 449 us -> 259 us (0.58)
  waiting for transfers between devices: 341 us -> 0 us
  Pallas kernels: 76.4 us -> 245 us
  between operations: 13.8 us -> 0.69 us
  other arithmetic: 7.46 us -> 2.62 us
    pallas_call x1, Pallas kernels: 76.4 us -> 245 us  [body(): pl.pallas_call(functools.partial(kernel, section_count, micro_count, slot...]
    reduce_scatter x2 -> x0, waiting for transfers between devices: 152 us -> none  [the longest x1 76.6 us: body(): lax.psum_scatter(grad_in, 'dp', scatter_dimension=0, tiled=True)]
    all_gather x2 -> x0, waiting for transfers between devices: 121 us -> none  [the longest x1 62.8 us: body(): second_full = lax.all_gather(weight_out[0], 'dp', axis=0, tiled=True)]
    psum x1 -> x0, waiting for transfers between devices: 66 us -> none  [body(): small_total = lax.psum(small, 'dp')]
  transfers between devices with their start and end apart: 5 -> 0, of which waited for: 5 -> 0; matrix products, arithmetic and copies ran while one was open for 3% -> 0% of each run, Pallas kernels for 0% -> 0%
where the time goes in v3:
time: 259 us
  Pallas kernels  245 us (95%)
  local copies, waits for them, and re-layouts  10.6 us (4%)
  other arithmetic  2.62 us (1%)
    pallas_call x1, Pallas kernels, body(): pl.pallas_call(functools.partial(kernel, section_count, micro_count, slot...  245 us
    unnamed x10, local copies, waits for them, and re-layouts  5.43 us

profile of v3, /device:TPU:0, one launch (start us, length us, event | category | flops | bytes accessed | tf_op | source)
XLA Modules:
  0.0 258.7 jit_solution(9461177824027839485)
XLA Ops:
  0.6 0.0 copy-start.2
  0.6 0.0 copy-start.1
  0.7 1.3 broadcast_in_dim.54.head_ref
  2.0 0.7 fusion
  2.7 0.1 broadcast_in_dim.51
  2.8 0.1 broadcast_in_dim.52
  2.9 0.1 mul.13
  3.0 0.1 mul.14
  3.1 0.0 copy-done.2
  3.1 0.1 convert_element_type.29
  3.2 1.6 copy.15
  4.8 0.9 select_add_fusion.own_labels
  5.7 0.0 copy-done.1
  5.7 1.0 broadcast_multiply_fusion.x_ref
  6.6 244.8 %shard_map.110 = (f32[80,2560]{1,0:T(8,128)}, f32[320,640]{1,0:T(8,128)}, f32[64,640]{1,0:T(8,128)}) custom-call(bf16[4,128,640]{2,1,0:T(8,128)(2,1)} %broadcast_multiply_fusion.x_ref, f32[4,128,128]{2,1,0:T(8,128)} %select_add_fusion.own_labels, f32[49,640]{1,0:T(8,128)} %bitcast.19, bf16[80,2560]{1,0:T(8,128)(2,1)} %bitcast.21, bf16[320,640]{1,0:T(8,128)(2,1)} %bitcast.22, ...), custom_call_target="tpu_custom_call" | custom-call | flops 10066329600 | bytes 13107200 | tf_op jit(solution)/shard_map/pallas_call | solution.py:814
  251.4 1.2 slice.11
  252.6 1.3 slice_reduce_fusion
  254.0 0.9 slice_bitcast_fusion
  254.9 0.8 copy.12
  255.7 0.0 copy-start
  255.7 2.2 copy.18
  257.8 0.0 copy-done
  257.8 0.9 copy.19
  (2 shorter events, 0.0 us)
Async XLA Ops:
  0.6 2.4 copy-start.2
  0.6 5.0 %copy-start.1 = (bf16[1,4,2,8,8,640]{5,4,3,2,1,0:T(8,128)(2,1)S(1)}, bf16[1,4,2,8,8,640]{5,4,3,2,1,0:T(8,128)(2,1)}, u32[]{:S(2)}) copy-start(bf16[1,4,2,8,8,640]{5,4,3,2,1,0:T(8,128)(2,1)} %param.7) | copy-start | bytes 1966084
  255.7 2.2 copy-start

commit v4 on v3

--- a/solution.py
+++ b/solution.py
@@ -59,6 +59,7 @@
         self.role = self.swap(self.along)
         self.role_row, self.role_core = lax.rem(self.along, 2), self.along // 2
         self.keeper = self.home == self.role
+        self.lands = (self.row == self.role_row, self.row != self.role_row)
 
     def swap(self, index):
         return 2 * lax.rem(index, 2) + index // 2
@@ -106,11 +107,12 @@
         target = self.shard(which, place.group)
         return remote(
             self.weights[which][0], target, self.first_send.at[which],
-            self.recv.at[which, place.group], place.at(along=plane, core=which),
+            self.recv.at[which, place.group],
+            place.at(along=plane, core=which, row=place.row if which == 0 else 1 - place.row),
         )
 
     def stays(self, which):
-        return self.place.keeper & (self.place.core == which)
+        return self.place.keeper & (self.place.core == which) & self.place.lands[which]
 
     def spread(self, which, origin, sem, device):
         target = self.shard(which, origin)
@@ -152,7 +154,6 @@
 
     def run(self):
         place = self.place
-        in_row = place.row == place.role_row
         for which in range(2):
 
             @pl.when(place.core == which)
@@ -162,14 +163,14 @@
                     origin = 2 * along + place.across
                     if turn == 0:
 
-                        @pl.when(jnp.logical_not(place.keeper))
+                        @pl.when(jnp.logical_not(self.stays(which)))
                         def _():
                             self.to_core(which, origin).wait_recv()
                     else:
                         self.to_core(which, origin).wait_recv()
                     self.to_across(which, along).start()
 
-                    @pl.when(in_row)
+                    @pl.when(place.lands[which])
                     def _():
                         self.to_row(which, along).start()
 
@@ -199,7 +200,7 @@
                 for along in range(4):
                     self.to_across(which, along).wait_send()
 
-                    @pl.when(place.row == place.role_row)
+                    @pl.when(place.lands[which])
                     def _():
                         self.to_row(which, along).wait_send()
 
@@ -247,12 +248,12 @@
         source = slab(self.sums[which], 2 * along + place.across, self.height(which))
         return remote(
             source, self.homes[which], self.home_send.at[along], self.home_recv.at[which],
-            place.at(along=along, core=place.role_core),
+            place.at(along=along, core=place.role_core, row=place.role_row),
         )
 
     def goes(self, along):
         place = self.place
-        return (along != place.along) | (place.core != place.role_core)
+        return (along != place.along) | jnp.logical_not(place.keeper)
 
     def add(self, which, along, count, first, buffer):
         height = count * self.height(which)
@@ -281,8 +282,8 @@
     def over_plane(self, turn):
         place = self.place
         along = place.far_first(turn)
-        in_row = place.row == place.role_row
         for which in range(2):
+            in_row = place.lands[which]
 
             @pl.when(place.core == which)
             def _():
@@ -312,7 +313,7 @@
     def finish(self, outputs):
         place = self.place
         for which in range(2):
-            here = place.keeper & (place.core == which)
+            here = place.keeper & (place.core == which) & place.lands[which]
 
             @pl.when(jnp.logical_not(here))
             def _():
@@ -322,8 +323,8 @@
 
     def wait_sends(self):
         place = self.place
-        in_row = place.row == place.role_row
         for which in range(2):
+            in_row = place.lands[which]
             for along in range(4):
 
                 @pl.when(place.core != which)
@@ -356,13 +357,11 @@
     if inside:
         place = Place()
         section = place.role
-        peers = [place.at(along=lax.rem(place.along + step, 4)) for step in range(1, 4)]
-        peers += [
-            place.at(along=lax.rem(place.along + step, 4), core=1 - place.core)
-            for step in range(4)
+        peers = [
+            {"dp": 2 * lax.rem(place.along + along, 4) + place.across,
+             "section": lax.rem(place.home + other, 4)}
+            for along in range(4) for other in range(4) if along + other > 0
         ]
-        peers += [place.at(row=1 - place.row)]
-        peers += [place.at(row=1 - place.row, core=1 - place.core)]
         peers += [place.at(across=1 - place.across)]
     else:
         section = lax.axis_index("section")

time: 259 us -> 235 us (0.907)
  Pallas kernels: 245 us -> 221 us
    pallas_call x1, Pallas kernels: 245 us -> 221 us  [body(): pl.pallas_call(functools.partial(kernel, section_count, micro_count, slot...]
where the time goes in v4:
time: 235 us; the launch traced here: 234 us
  Pallas kernels  221 us (94%)
  local copies, waits for them, and re-layouts  10.6 us (5%)
  other arithmetic  2.62 us (1%)
    pallas_call x1, Pallas kernels, body(): pl.pallas_call(functools.partial(kernel, section_count, micro_count, slot...  221 us
    unnamed x10, local copies, waits for them, and re-layouts  5.43 us

profile of v4, /device:TPU:0, one launch (start us, length us, event | category | flops | bytes accessed | tf_op | source)
XLA Modules:
  0.0 234.4 jit_solution(8984135339349865237)
XLA Ops:
  0.6 0.0 copy-start.2
  0.6 0.0 copy-start.1
  0.7 1.3 broadcast_in_dim.54.head_ref
  2.0 0.7 fusion
  2.7 0.1 broadcast_in_dim.51
  2.8 0.1 broadcast_in_dim.52
  2.9 0.1 mul.13
  3.0 0.1 mul.14
  3.1 0.0 copy-done.2
  3.1 0.1 convert_element_type.29
  3.2 1.6 copy.15
  4.8 0.9 select_add_fusion.own_labels
  5.7 0.0 copy-done.1
  5.7 1.0 broadcast_multiply_fusion.x_ref
  6.6 220.5 %shard_map.110 = (f32[80,2560]{1,0:T(8,128)}, f32[320,640]{1,0:T(8,128)}, f32[64,640]{1,0:T(8,128)}) custom-call(bf16[4,128,640]{2,1,0:T(8,128)(2,1)} %broadcast_multiply_fusion.x_ref, f32[4,128,128]{2,1,0:T(8,128)} %select_add_fusion.own_labels, f32[49,640]{1,0:T(8,128)} %bitcast.19, bf16[80,2560]{1,0:T(8,128)(2,1)} %bitcast.21, bf16[320,640]{1,0:T(8,128)(2,1)} %bitcast.22, ...), custom_call_target="tpu_custom_call" | custom-call | flops 10066329600 | bytes 13107200 | tf_op jit(solution)/shard_map/pallas_call | solution.py:813
  227.2 1.2 slice.11
  228.3 1.3 slice_reduce_fusion
  229.7 0.9 slice_bitcast_fusion
  230.6 0.8 copy.12
  231.4 0.0 copy-start
  231.4 2.2 copy.18
  233.5 0.0 copy-done
  233.5 0.9 copy.19
  (2 shorter events, 0.0 us)
Async XLA Ops:
  0.6 2.4 %copy-start.2 = (s32[1,4,2,8,8]{4,3,2,1,0:T(8,128)S(1)}, s32[1,4,2,8,8]{4,3,2,1,0:T(8,128)}, u32[]{:S(2)}) copy-start(s32[1,4,2,8,8]{4,3,2,1,0:T(8,128)} %param.8) | copy-start | bytes 6148
  0.6 5.0 %copy-start.1 = (bf16[1,4,2,8,8,640]{5,4,3,2,1,0:T(8,128)(2,1)S(1)}, bf16[1,4,2,8,8,640]{5,4,3,2,1,0:T(8,128)(2,1)}, u32[]{:S(2)}) copy-start(bf16[1,4,2,8,8,640]{5,4,3,2,1,0:T(8,128)(2,1)} %param.7) | copy-start | bytes 1966084
  231.4 2.2 copy-start

commit v5 on v4

--- a/solution.py
+++ b/solution.py
@@ -131,10 +131,10 @@
             place.at(across=1 - place.across),
         )
 
-    def to_row(self, which, along):
+    def to_row(self, which, origin):
         place = self.place
         return self.spread(
-            which, 2 * along + place.across, self.row_send.at[along], place.at(row=1 - place.row)
+            which, origin, self.row_send.at[origin], place.at(row=1 - place.row)
         )
 
     def start(self):
@@ -168,16 +168,25 @@
                             self.to_core(which, origin).wait_recv()
                     else:
                         self.to_core(which, origin).wait_recv()
-                    self.to_across(which, along).start()
+                    if turn < 2:
+                        self.to_across(which, along).start()
 
                     @pl.when(place.lands[which])
                     def _():
-                        self.to_row(which, along).start()
+                        if turn >= 2:
+                            self.to_across(which, along).start()
+                        self.to_row(which, origin).start()
 
                     self.to_core(which, origin).start()
                 for turn in range(4):
                     origin = 2 * place.near_first(turn) + 1 - place.across
                     self.to_core(which, origin).wait_recv()
+                    if turn >= 2:
+
+                        @pl.when(place.lands[which])
+                        def _():
+                            self.to_row(which, origin).start()
+
                     self.to_core(which, origin).start()
 
         for which in range(2):
@@ -197,12 +206,17 @@
 
             @pl.when(place.core == which)
             def _():
-                for along in range(4):
-                    self.to_across(which, along).wait_send()
+                for turn in range(4):
+                    along = place.near_first(turn)
+                    if turn < 2:
+                        self.to_across(which, along).wait_send()
 
                     @pl.when(place.lands[which])
                     def _():
-                        self.to_row(which, along).wait_send()
+                        self.to_row(which, 2 * along + place.across).wait_send()
+                        if turn >= 2:
+                            self.to_across(which, along).wait_send()
+                            self.to_row(which, 2 * along + 1 - place.across).wait_send()
 
                 for origin in range(8):
                     self.to_core(which, origin).wait_send()
@@ -805,7 +819,7 @@
             pltpu.VMEM((SMALL_ROWS, width), full),
             pltpu.VMEM(depth_kernels.shape[1:], full),
             pltpu.VMEM(labels.shape, full),
-            dma((2, 8)), dma((2,)), dma((8,)), dma((4,)), dma((4,)),
+            dma((2, 8)), dma((2,)), dma((8,)), dma((4,)), dma((8,)),
             dma((4,)), dma((4,)), dma((4,)), dma((4,)), dma((4,)), dma((4,)), dma((4,)), dma((2,)),
             dma((3,)), dma((3,)), dma((3,)), dma, dma((micro_count,)), dma, dma,
             dma((3,)), dma,

time: 235 us -> 237 us (level)
  no operation moved by 1% of the time
where the time goes in v5:
time: 237 us
  Pallas kernels  223 us (94%)
  local copies, waits for them, and re-layouts  10.6 us (4%)
  other arithmetic  2.62 us (1%)
    pallas_call x1, Pallas kernels, body(): pl.pallas_call(functools.partial(kernel, section_count, micro_count, slot...  223 us
    unnamed x10, local copies, waits for them, and re-layouts  5.43 us

profile of v5, /device:TPU:0, one launch (start us, length us, event | category | flops | bytes accessed | tf_op | source)
XLA Modules:
  0.0 236.6 jit_solution(4737938469260234026)
XLA Ops:
  0.6 0.0 copy-start.2
  0.6 0.0 copy-start.1
  0.7 1.3 broadcast_in_dim.54.head_ref
  2.0 0.7 fusion
  2.7 0.1 broadcast_in_dim.51
  2.8 0.1 broadcast_in_dim.52
  2.9 0.1 mul.13
  3.0 0.1 mul.14
  3.1 0.0 copy-done.2
  3.1 0.1 convert_element_type.29
  3.2 1.6 copy.15
  4.8 0.9 select_add_fusion.own_labels
  5.7 0.0 copy-done.1
  5.7 1.0 broadcast_multiply_fusion.x_ref
  6.6 222.7 %shard_map.110 = (f32[80,2560]{1,0:T(8,128)}, f32[320,640]{1,0:T(8,128)}, f32[64,640]{1,0:T(8,128)}) custom-call(bf16[4,128,640]{2,1,0:T(8,128)(2,1)} %broadcast_multiply_fusion.x_ref, f32[4,128,128]{2,1,0:T(8,128)} %select_add_fusion.own_labels, f32[49,640]{1,0:T(8,128)} %bitcast.19, bf16[80,2560]{1,0:T(8,128)(2,1)} %bitcast.21, bf16[320,640]{1,0:T(8,128)(2,1)} %bitcast.22, ...), custom_call_target="tpu_custom_call" | custom-call | flops 10066329600 | bytes 13107200 | tf_op jit(solution)/shard_map/pallas_call | solution.py:827
  229.3 1.2 slice.11
  230.5 1.3 slice_reduce_fusion
  231.8 0.9 slice_bitcast_fusion
  232.7 0.8 copy.12
  233.5 0.0 copy-start
  233.5 2.2 copy.18
  235.7 0.0 copy-done
  235.7 0.9 copy.19
  (2 shorter events, 0.0 us)
Async XLA Ops:
  0.6 2.4 %copy-start.2 = (s32[1,4,2,8,8]{4,3,2,1,0:T(8,128)S(1)}, s32[1,4,2,8,8]{4,3,2,1,0:T(8,128)}, u32[]{:S(2)}) copy-start(s32[1,4,2,8,8]{4,3,2,1,0:T(8,128)} %param.8) | copy-start | bytes 6148
  0.6 5.0 %copy-start.1 = (bf16[1,4,2,8,8,640]{5,4,3,2,1,0:T(8,128)(2,1)S(1)}, bf16[1,4,2,8,8,640]{5,4,3,2,1,0:T(8,128)(2,1)}, u32[]{:S(2)}) copy-start(bf16[1,4,2,8,8,640]{5,4,3,2,1,0:T(8,128)(2,1)} %param.7) | copy-start | bytes 1966084
  233.5 2.2 copy-start
